TPU v7x, 32 devices: a whole 2x2x4 slice. The times are simulated.
32 devices in a mesh: blk: 8 (over y, x, core), head: 4 (over z).
Axes of the slice: x: 2, y: 2, z: 4, core: 2. Of those that a mesh axis runs over, the one named last changes fastest.
Arguments:
- hidden_in: bfloat16 [4096, 2048], P('blk'), may hold values from -6 to 6
- layer_input: bfloat16 [4096, 256], P(('blk', 'head')), may hold values from -6 to 6
- in_gain: float32 [2048], replicated, may hold values from 0.5 to 1.5
- w_query: bfloat16 [2048, 2048], P(None, 'head'), may hold values from -0.125 to 0.125
- w_keyval: bfloat16 [2048, 1024], P(None, 'head'), may hold values from -0.125 to 0.125
- q_gain: float32 [256], replicated, may hold values from 0.2 to 0.45
- k_gain: float32 [256], replicated, may hold values from 0.2 to 0.45
- w_out: bfloat16 [2048, 2048], P('head'), may hold values from -0.125 to 0.125
- post_gain: float32 [2048], replicated, may hold values from 0.5 to 1.5
- laurel_left: bfloat16 [2048, 64], replicated, may hold values from -0.125 to 0.125
- laurel_right: bfloat16 [64, 2048], replicated, may hold values from -0.75 to 0.75
- laurel_gain: float32 [2048], replicated, may hold values from 0.5 to 1.5
- w_plgate: bfloat16 [2048, 256], replicated, may hold values from -0.125 to 0.125
- w_plproj: bfloat16 [256, 2048], replicated, may hold values from -0.375 to 0.375
- pl_gain: float32 [2048], replicated, may hold values from 0.5 to 1.5
- kv_pool: bfloat16 [96, 4, 128, 256], P('blk'), may hold values from -44 to 44, as said below
- page_table: int32 [8, 12], P('blk'), may hold values from 0 to 11, each once within a row
- prefix_len: int32 [8], P('blk'), may hold values from 1 to 1536, as said below
- decode_owner: int32 [8], replicated, may hold values from 0 to 7, each once
Outputs:
- mixed: bfloat16 [4096, 2048], P(('blk', 'head'))
- decode_kv: bfloat16 [4, 8, 2048, 256], P('head', 'blk')
Inputs may be any that keep to these rules, and one draw needn't show every extreme that they name: `kv_pool`: cached keys and values; one request's prefix fills its 12 pages in every draw. `page_table`: each row names each of its 12 pool pages once. `prefix_len`: some request has exactly 1536 cached tokens. `decode_owner`: each request has its own slot.
All inputs are finite; a program needn't handle non-finite values.
Results may differ from a plain program's by a relative error of at most 0.009.
Values may be sent and summed in bfloat16 or wider, within the bound.
A program may use at most 128 MiB of HBM per device.

v0:
```python
import jax
import jax.numpy as jnp
from jax import lax
from jax.sharding import PartitionSpec as P

QH = 8
KVH = 2


eps = 1e-06
rope_base = 1000000.0


def rms_scale(values):
    return values * lax.rsqrt(jnp.mean(values * values, axis=-1, keepdims=True) + eps)


def rotate(values, positions):
    half_dim = values.shape[-1] // 2
    frequency = rope_base ** (-jnp.arange(half_dim, dtype=jnp.float32) / half_dim)
    angles = positions.astype(jnp.float32)[:, None] * frequency[None, :]
    cosine = jnp.cos(angles)
    sine_part = jnp.sin(angles)
    lower_half = values[..., :half_dim]
    upper_half = values[..., half_dim:]
    return jnp.concatenate(
        [
            lower_half * cosine - upper_half * sine_part,
            upper_half * cosine + lower_half * sine_part,
        ],
        axis=-1,
    )


def scores_of(rows, keys):
    return lax.dot_general(rows, keys, (((1,), (1,)), ((), ())), preferred_element_type=jnp.float32)


def on_device(
    hidden_in,
    layer_input,
    in_gain,
    w_query,
    w_keyval,
    q_gain,
    k_gain,
    w_out,
    post_gain,
    laurel_left,
    laurel_right,
    laurel_gain,
    w_plgate,
    w_plproj,
    pl_gain,
    kv_pool,
    page_table,
    prefix_len,
    decode_owner,
):
    new_rows = hidden_in.shape[0]
    head_dim = kv_pool.shape[3]
    page_len = kv_pool.shape[2]
    n_pages = page_table.shape[1]
    kv_heads = kv_pool.shape[1] // 2
    local_heads = w_query.shape[1] // head_dim
    prefix_max = n_pages * page_len
    total_len = prefix_max + new_rows
    blocks = lax.axis_size("blk")
    block_span = total_len // blocks
    head_idx = lax.axis_index("head")
    kv_of = head_idx * local_heads // (QH // KVH)
    length = prefix_len[0]
    positions = length + jnp.arange(new_rows, dtype=jnp.int32)
    my_pages = jnp.take(kv_pool, page_table[0], axis=0)
    live_mask = jnp.arange(prefix_max, dtype=jnp.int32) < length
    own_old = lax.dynamic_index_in_dim(my_pages, head_idx, 1, keepdims=False).reshape(
        prefix_max, head_dim
    )
    own_old = jnp.where(live_mask[:, None], own_old, jnp.zeros_like(own_old))
    old_part = jnp.concatenate([own_old, jnp.zeros((new_rows, head_dim), jnp.bfloat16)], axis=0)
    normed = (rms_scale(hidden_in.astype(jnp.float32)) * in_gain).astype(jnp.bfloat16)
    queries = jnp.dot(normed, w_query, preferred_element_type=jnp.float32).reshape(
        new_rows, local_heads, head_dim
    )
    queries = rotate(jnp.transpose(rms_scale(queries) * q_gain, (1, 0, 2)), positions).astype(
        jnp.bfloat16
    )
    own_proj = rms_scale(jnp.dot(normed, w_keyval, preferred_element_type=jnp.float32))
    fresh_slot = jnp.where(
        head_idx < kv_heads, rotate(own_proj * k_gain, positions), own_proj
    ).astype(jnp.bfloat16)
    gathered = lax.all_gather(fresh_slot[None], "head", axis=0, tiled=True)
    new_key = lax.dynamic_index_in_dim(gathered, kv_of, 0, keepdims=False)
    new_val = lax.dynamic_index_in_dim(gathered, kv_of + kv_heads, 0, keepdims=False)
    pre_key = lax.dynamic_index_in_dim(my_pages, kv_of, 1, keepdims=False).reshape(
        prefix_max, head_dim
    )
    pre_val = lax.dynamic_index_in_dim(my_pages, kv_of + kv_heads, 1, keepdims=False).reshape(
        prefix_max, head_dim
    )
    flat_q = queries.reshape(local_heads * new_rows, head_dim)
    row_pos = jnp.tile(jnp.arange(new_rows, dtype=jnp.int32), local_heads)
    causal = jnp.arange(new_rows, dtype=jnp.int32)[None, :] <= row_pos[:, None]
    new_scores = jnp.where(causal, scores_of(flat_q, new_key), -jnp.inf)
    old_scores = jnp.where(live_mask[None, :], scores_of(flat_q, pre_key), -jnp.inf)
    row_top = jnp.maximum(jnp.max(old_scores, axis=1), jnp.max(new_scores, axis=1))
    old_exp = jnp.exp(old_scores - row_top[:, None])
    new_exp = jnp.exp(new_scores - row_top[:, None])
    row_total = jnp.sum(old_exp, axis=1) + jnp.sum(new_exp, axis=1)
    weighted = jnp.dot(old_exp.astype(jnp.bfloat16), pre_val, preferred_element_type=jnp.float32)
    weighted = weighted + jnp.dot(
        new_exp.astype(jnp.bfloat16), new_val, preferred_element_type=jnp.float32
    )
    attn = (
        (weighted / row_total[:, None])
        .astype(jnp.bfloat16)
        .reshape(local_heads, new_rows, head_dim)
    )
    attn = jnp.transpose(attn, (1, 0, 2)).reshape(new_rows, local_heads * head_dim)
    quarter = new_rows // lax.axis_size("head")
    row_start = head_idx * quarter
    proj_rows = lax.psum_scatter(
        jnp.dot(attn, w_out, preferred_element_type=jnp.float32).astype(jnp.bfloat16),
        "head",
        scatter_dimension=0,
        tiled=True,
    ).astype(jnp.float32)
    tokens_rows = lax.dynamic_slice_in_dim(hidden_in, row_start, quarter, 0).astype(jnp.float32)
    normed_rows = lax.dynamic_slice_in_dim(normed, row_start, quarter, 0)
    branch_low = jnp.dot(normed_rows, laurel_left, preferred_element_type=jnp.float32).astype(
        jnp.bfloat16
    )
    laurel = (
        normed_rows.astype(jnp.float32)
        + rms_scale(jnp.dot(branch_low, laurel_right, preferred_element_type=jnp.float32))
        * laurel_gain
    )
    state = (tokens_rows + rms_scale(proj_rows) * post_gain + laurel) * 2.0 ** (-0.5)
    state_b = state.astype(jnp.bfloat16)
    gated = (
        jax.nn.gelu(
            jnp.dot(state_b, w_plgate, preferred_element_type=jnp.float32), approximate=True
        )
        * layer_input.astype(jnp.float32)
    ).astype(jnp.bfloat16)
    mixed = (
        state + rms_scale(jnp.dot(gated, w_plproj, preferred_element_type=jnp.float32)) * pl_gain
    ).astype(jnp.bfloat16)
    full_seq = lax.dynamic_update_slice(old_part, fresh_slot, (length, jnp.int32(0)))
    spread = lax.all_to_all(
        full_seq.reshape(blocks, block_span, head_dim),
        "blk",
        split_axis=0,
        concat_axis=0,
        tiled=True,
    )
    inverse = (
        jnp.zeros((blocks,), jnp.int32).at[decode_owner].set(jnp.arange(blocks, dtype=jnp.int32))
    )
    arranged = jnp.take(spread, inverse, axis=0)
    owned = lax.all_to_all(arranged, "blk", split_axis=0, concat_axis=0, tiled=True)
    return (mixed, owned.reshape(1, 1, total_len, head_dim))


def solution(mesh):
    in_specs = (
        P("blk", None),
        P(("blk", "head"), None),
        P(),
        P(None, "head"),
        P(None, "head"),
        P(),
        P(),
        P("head", None),
        P(),
        P(),
        P(),
        P(),
        P(),
        P(),
        P(),
        P("blk", None, None, None),
        P("blk", None),
        P("blk"),
        P(),
    )
    out_specs = (P(("blk", "head"), None), P("head", "blk", None, None))
    return jax.shard_map(
        on_device, mesh=mesh, in_specs=in_specs, out_specs=out_specs, check_vma=False
    )
```

profile of v0, /device:TPU:0, one launch (start us, length us, event | category | flops | bytes accessed | tf_op | source)
XLA Modules:
  0.0 132.7 jit_solution(17632277822654272188)
XLA Ops:
  8.1 2.2 %fusion.2 = f32[512]{0:T(512)S(1)} fusion(bf16[512,2048]{1,0:T(8,128)(2,1)} %param.19), kind=kLoop, calls=%fused_computation.9 | loop fusion | flops 3145216 | bytes 2099200 | tf_op jit(solution)/shard_map/reduce_sum | solution.py:15
  17.4 4.5 %multiply_reduce_fusion.2 = (f32[512,2]{0,1:T(2,128)S(1)}, f32[512,512]{0,1:T(8,128)}) fusion(bf16[512,2048]{1,0:T(8,128)(2,1)} %copy-done.3, bf16[2048,512]{1,0:T(8,128)(2,1)} %param.22), kind=kOutput, calls=%fused_computation.43 | convolution fusion | flops 1074265088 | bytes 5246976 | tf_op jit(solution)/shard_map/dot_general | solution.py:82
  21.9 2.5 %copy.23 = f32[512,2,256]{2,0,1:T(8,128)} copy(f32[512,2,256]{0,2,1:T(8,128)} %bitcast.54) | data formatting | bytes 2097152 | tf_op jit(solution)/shard_map/reshape | solution.py:82
  24.5 2.5 %gather_fusion = bf16[12,4,128,256]{3,2,1,0:T(8,128)(2,1)} fusion(bf16[12,4,128,256]{3,2,1,0:T(8,128)(2,1)S(1)} %copy-done, s32[1024]{0:T(1024)S(1)} %pad_clamp_fusion.1), kind=kCustom, calls=%fused_computation | custom fusion | bytes 6291504 | tf_op jit(solution)/shard_map/jit(_take)/gather | solution.py:74
  27.0 4.0 %broadcast_select_fusion = bf16[12,4,128,256]{3,2,1,0:T(8,128)(2,1)} fusion(bf16[12,4,128,256]{3,2,1,0:T(8,128)(2,1)} %gather_fusion, pred[12]{0:T(512)(128)(4,1)S(1)} %compare_and_fusion.1), kind=kLoop, calls=%fused_computation.15 | loop fusion | flops 1572864 | bytes 6291468 | tf_op jit(solution)/shard_map/jit(_take)/select_n | solution.py:74
  31.0 3.0 %constant_dynamic-slice_fusion = (bf16[12,1,128,256]{3,2,1,0:T(8,128)(2,1)}, bf16[12,1,128,256]{3,2,1,0:T(8,128)(2,1)}, bf16[12,1,128,256]{3,2,1,0:T(8,128)(2,1)S(1)}) fusion(bf16[12,4,128,256]{3,2,1,0:T(8,128)(2,1)} %broadcast_select_fusion, s32[]{:T(128)S(6)} %select_n.90, s32[]{:T(128)S(6)} %select_n.87, s32[]{:T(128)S(6)} %select_n.82), kind=kLoop, calls=%fused_computation.96 | loop fusion | bytes 4718604 | tf_op jit(solution)/shard_map/jit(dynamic_index_in_dim)/dynamic_slice | solution.py:76
  36.1 3.7 %select_reduce_fusion = (f32[1024]{0:T(1024)S(1)}, f32[1024,1536]{1,0:T(8,128)}) fusion(pred[1536]{0:T(1024)(128)(4,1)S(1)} %iota_compare_fusion.1, bf16[1536,256]{1,0:T(8,128)(2,1)S(1)} %bitcast.53, bf16[1024,128]{1,0:T(8,128)(2,1)S(1)} %bitcast.57, bf16[1024,128]{1,0:T(8,128)(2,1)S(1)} %bitcast.55), kind=kOutput, calls=%fused_computation.4 | convolution fusion | flops 809499648 | bytes 7607808 | tf_op jit(solution)/shard_map/dot_general | solution.py:36
  39.8 8.1 %all-gather.3.cloned.1.call-done = bf16[2048,256]{1,0:T(8,128)(2,1)} async-done(((bf16[512,256]{1,0:T(8,128)(2,1)}), bf16[2048,256]{1,0:T(8,128)(2,1)}) %all-gather.3.cloned.1.call-update) | async-done | bytes 1048592 | tf_op jit(solution)/shard_map/all_gather | solution.py:92
  47.9 1.6 %fusion.11 = (f32[1024]{0:T(1024)S(1)}, f32[1024,512]{0,1:T(8,128)S(1)}) fusion(s32[1024]{0:T(1024)S(1)} %bitcast.62, bf16[4,512,256]{2,1,0:T(8,128)(2,1)} %bitcast.65, s32[]{:T(128)S(6)} %select_n.82, bf16[1024,128]{1,0:T(8,128)(2,1)} %bitcast.58, bf16[1024,128]{1,0:T(8,128)(2,1)S(1)} %bitcast.56), kind=kOutput, calls=%fused_computation.21 | convolution fusion | flops 271055872 | bytes 2891780 | tf_op jit(solution)/shard_map/dot_general | solution.py:36
  49.5 4.1 %fusion = f32[1024]{0:T(1024)S(1)} fusion(f32[1024,1536]{1,0:T(8,128)} %get-tuple-element.14, f32[1024]{0:T(1024)S(1)} %max.7, pred[1536]{0:T(1024)(128)(4,1)S(1)} %iota_compare_fusion.1), kind=kLoop, calls=%fused_computation.7 | loop fusion | flops 4717568 | bytes 6301184 | tf_op jit(solution)/shard_map/reduce_sum | solution.py:109
  55.8 2.5 %fusion.15 = bf16[1024,256]{1,0:T(8,128)(2,1)} fusion(f32[1024,256]{1,0:T(8,128)S(1)} %fusion.5, f32[1024,512]{0,1:T(8,128)S(1)} %get-tuple-element.18, f32[1024]{0:T(1024)S(1)} %max.7, s32[1024]{0:T(1024)S(1)} %bitcast.64, f32[1024]{0:T(1024)S(1)} %add.166, bf16[4,512,256]{2,1,0:T(8,128)(2,1)} %bitcast.66, s32[]{:T(128)S(6)} %select_n.87), kind=kOutput, calls=%fused_computation.28 | convolution fusion | flops 271319040 | bytes 3944452 | tf_op jit(solution)/shard_map/dot_general | solution.py:111
  58.2 2.0 %copy.24 = bf16[2,512,256]{1,2,0:T(8,128)(2,1)} copy(bf16[2,512,256]{2,1,0:T(8,128)(2,1)} %bitcast.60) | data formatting | bytes 1048576 | tf_op jit(solution)/shard_map/reshape | solution.py:117
  60.3 4.4 %convolution_convert_fusion = bf16[512,2048]{1,0:T(8,128)(2,1)} fusion(bf16[512,512]{0,1:T(8,128)(2,1)} %bitcast.61, bf16[512,2048]{1,0:T(8,128)(2,1)} %param.26), kind=kOutput, calls=%fused_computation.17 | convolution fusion | flops 1074790400 | bytes 4718592 | tf_op jit(solution)/shard_map/dot_general | solution.py:123
  67.2 2.8 %dynamic_update_slice.3 = bf16[2048,256]{1,0:T(8,128)(2,1)} dynamic-update-slice(bf16[2048,256]{1,0:T(8,128)(2,1)} %concatenate.19, bf16[512,256]{1,0:T(8,128)(2,1)S(1)} %copy-done.5, s32[]{:T(128)S(6)} %select_n.92, s32[]{:T(128)} %constant.53.clone.1) | dynamic-update-slice | bytes 524292 | tf_op jit(solution)/shard_map/dynamic_update_slice | solution.py:149
  70.0 4.2 %all-to-all-start = ((bf16[8,256,256]{2,1,0:T(8,128)(2,1)}), bf16[8,256,256]{2,1,0:T(8,128)(2,1)}, u32[]{:S(2)}, u32[]{:S(2)}) async-start(bf16[8,256,256]{2,1,0:T(8,128)(2,1)} %bitcast.52), calls=%async_computation.1 | async-start | bytes 2097152 | tf_op jit(solution)/shard_map/all_to_all | solution.py:150
  74.9 14.7 %all-to-all-done = bf16[8,256,256]{2,1,0:T(8,128)(2,1)} async-done(((bf16[8,256,256]{2,1,0:T(8,128)(2,1)}), bf16[8,256,256]{2,1,0:T(8,128)(2,1)}, u32[]{:S(2)}, u32[]{:S(2)}) %all-to-all-start) | async-done | bytes 1048608 | tf_op jit(solution)/shard_map/all_to_all | solution.py:150
  89.6 2.8 %gather_fusion.1 = bf16[8,256,256]{2,1,0:T(8,128)(2,1)} fusion(bf16[8,256,256]{2,1,0:T(8,128)(2,1)} %all-to-all-done, s32[1024]{0:T(1024)S(1)} %pad_clamp_fusion), kind=kCustom, calls=%fused_computation.1 | custom fusion | bytes 2097184 | tf_op jit(solution)/shard_map/jit(_take)/gather | solution.py:160
  92.5 2.4 %broadcast_select_fusion.1 = bf16[8,256,256]{2,1,0:T(8,128)(2,1)} fusion(bf16[8,256,256]{2,1,0:T(8,128)(2,1)} %gather_fusion.1, pred[8]{0:T(512)(128)(4,1)S(1)} %compare_and_fusion), kind=kLoop, calls=%fused_computation.44 | loop fusion | flops 524288 | bytes 2097160 | tf_op jit(solution)/shard_map/jit(_take)/select_n | solution.py:160
  94.9 4.6 %all-to-all-start.1 = ((bf16[8,256,256]{2,1,0:T(8,128)(2,1)}), bf16[8,256,256]{2,1,0:T(8,128)(2,1)}, u32[]{:S(2)}, u32[]{:S(2)}) async-start(bf16[8,256,256]{2,1,0:T(8,128)(2,1)} %broadcast_select_fusion.1), calls=%async_computation.2 | async-start | bytes 2097152 | tf_op jit(solution)/shard_map/all_to_all | solution.py:161
  99.5 2.8 %multiply_reduce_fusion.1 = (f32[128]{0:T(128)S(1)}, f32[128,2048]{1,0:T(8,128)}) fusion(bf16[64,2048]{1,0:T(8,128)(2,1)S(1)} %copy-done.9, bf16[2048,64]{0,1:T(8,128)(2,1)} %param.28, bf16[512,2048]{1,0:T(8,128)(2,1)} %copy-done.3, s32[]{:T(128)S(6)} %select_n.77), kind=kOutput, calls=%fused_computation.38 | convolution fusion | flops 67641216 | bytes 2097668 | tf_op jit(solution)/shard_map/dot_general | solution.py:135
  102.3 12.3 %all-to-all-done.1 = bf16[8,256,256]{2,1,0:T(8,128)(2,1)} async-done(((bf16[8,256,256]{2,1,0:T(8,128)(2,1)}), bf16[8,256,256]{2,1,0:T(8,128)(2,1)}, u32[]{:S(2)}, u32[]{:S(2)}) %all-to-all-start.1) | async-done | bytes 1048608 | tf_op jit(solution)/shard_map/all_to_all | solution.py:161
  115.9 4.3 %multiply_reduce_fusion = (f32[128]{0:T(128)S(1)}, f32[128,2048]{1,0:T(8,128)}) fusion(bf16[256,2048]{1,0:T(8,128)(2,1)} %param.32, bf16[2048,256]{1,0:T(8,128)(2,1)} %param.31, bf16[128,256]{1,0:T(8,128)(2,1)S(1)} %copy-done.10, bf16[128,2048]{1,0:T(8,128)(2,1)} %reduce-scatter.2.cloned.1.call-done, f32[128,2048]{1,0:T(8,128)} %get-tuple-element.20, ...), kind=kOutput, calls=%fused_computation.37 | convolution fusion | flops 272465792 | bytes 5850628 | tf_op jit(solution)/shard_map/dot_general | solution.py:147
  120.2 3.4 %add_convert_fusion = bf16[128,2048]{1,0:T(8,128)(2,1)} fusion(f32[128,2048]{1,0:T(8,128)} %get-tuple-element.22, f32[2048]{0:T(1024)S(1)} %copy-done.14, f32[128]{0:T(128)S(1)} %add_rsqrt_fusion.3, f32[2048]{0:T(1024)S(1)} %copy-done.11, f32[128,2048]{1,0:T(8,128)} %get-tuple-element.20, f32[128]{0:T(128)S(1)} %add_rsqrt_fusion.4, ...), kind=kLoop, calls=%fused_computation.36 | loop fusion | flops 3932160 | bytes 4220420 | tf_op jit(solution)/shard_map/convert_element_type | solution.py:148
  123.6 2.3 %copy.29 = bf16[1,1,2048,256]{3,2,1,0:T(8,128)(2,1)} copy(bf16[1,1,2048,256]{3,2,1,0:T(8,128)(2,1)} %bitcast.18) | data formatting | bytes 2097152
  (80 shorter events, 15.7 us)
Async XLA Ops:
  7.2 17.3 %copy-start = (bf16[12,4,128,256]{3,2,1,0:T(8,128)(2,1)S(1)}, bf16[12,4,128,256]{3,2,1,0:T(8,128)(2,1)}, u32[]{:S(2)}) copy-start(bf16[12,4,128,256]{3,2,1,0:T(8,128)(2,1)} %param.34) | copy-start | bytes 9437188
  7.2 3.1 %copy-start.13 = (f32[2048]{0:T(1024)S(1)}, f32[2048]{0:T(1024)}, u32[]{:S(2)}) copy-start(f32[2048]{0:T(1024)} %param.21) | copy-start | bytes 24580
  7.2 40.7 %all-gather.3.cloned.1.call-start = ((), (), s32[]{:S(2)}) async-start(), calls=%async_computation.4 | async-start | bytes 1310720 | tf_op jit(solution)/shard_map/all_gather | solution.py:92
  7.3 3.1 %copy-start.2 = (bf16[512,2048]{1,0:T(8,128)(2,1)S(1)}, bf16[512,2048]{1,0:T(8,128)(2,1)}, u32[]{:S(2)}) copy-start(bf16[512,2048]{1,0:T(8,128)(2,1)} %param.19) | copy-start | bytes 6291460
  10.3 1.9 %copy-start.17 = (bf16[2048,256]{1,0:T(8,128)(2,1)S(1)}, bf16[2048,256]{1,0:T(8,128)(2,1)}, u32[]{:S(2)}) copy-start(bf16[2048,256]{1,0:T(8,128)(2,1)} %param.23) | copy-start | bytes 3145732
  10.9 1.4 %copy-start.3 = (bf16[512,2048]{1,0:T(8,128)(2,1)}, bf16[512,2048]{1,0:T(8,128)(2,1)S(1)}, u32[]{:S(2)}) copy-start(bf16[512,2048]{1,0:T(8,128)(2,1)S(1)} %fusion.4) | copy-start | bytes 6291460
  12.2 1.5 %copy-start.15 = (f32[256]{0:T(256)S(1)}, f32[256]{0:T(256)}, u32[]{:S(2)}) copy-start(f32[256]{0:T(256)} %param.25) | copy-start | bytes 3076
  13.8 3.6 %copy-start.18 = (s32[1,12]{1,0:T(1,128)S(1)}, s32[1,12]{1,0:T(1,128)}, u32[]{:S(2)}) copy-start(s32[1,12]{1,0:T(1,128)} %param.35) | copy-start | bytes 148
  13.8 2.5 %copy-start.6 = (f32[512,256]{1,0:T(8,128)S(1)}, f32[512,256]{1,0:T(8,128)}, u32[]{:S(2)}) copy-start(f32[512,256]{1,0:T(8,128)} %get-tuple-element.16) | copy-start | bytes 1572868
  17.1 97.6 %reduce-scatter.2.cloned.1.call-start = ((), (), s32[]{:S(2)}) async-start(), calls=%async_computation.3 | async-start | bytes 2621440 | tf_op jit(solution)/shard_map/reduce_scatter | solution.py:122
  31.0 4.1 %copy-start.4 = (f32[512,2,256]{2,0,1:T(8,128)S(1)}, f32[512,2,256]{2,0,1:T(8,128)}, u32[]{:S(2)}) copy-start(f32[512,2,256]{2,0,1:T(8,128)} %copy.23) | copy-start | bytes 3145732
  31.0 4.1 %copy-start.16 = (f32[256]{0:T(256)S(1)}, f32[256]{0:T(256)}, u32[]{:S(2)}) copy-start(f32[256]{0:T(256)} %param.24) | copy-start | bytes 3076
  35.4 0.7 copy-start.7
  47.9 5.7 %copy-start.8 = (bf16[12,1,128,256]{3,2,1,0:T(8,128)(2,1)S(1)}, bf16[12,1,128,256]{3,2,1,0:T(8,128)(2,1)}, u32[]{:S(2)}) copy-start(bf16[12,1,128,256]{3,2,1,0:T(8,128)(2,1)} %get-tuple-element.3) | copy-start | bytes 2359300
  49.5 4.6 %copy-start.1 = (f32[1024,1536]{1,0:T(8,128)S(1)}, f32[1024,1536]{1,0:T(8,128)}, u32[]{:S(2)}) copy-start(f32[1024,1536]{1,0:T(8,128)} %get-tuple-element.14) | copy-start | bytes 18874372
  64.7 2.5 %copy-start.5 = (bf16[512,256]{1,0:T(8,128)(2,1)S(1)}, bf16[512,256]{1,0:T(8,128)(2,1)}, u32[]{:S(2)}) copy-start(bf16[512,256]{1,0:T(8,128)(2,1)} %fusion.26) | copy-start | bytes 786436
  66.1 8.1 %copy-start.19 = (s32[8]{0:T(128)S(1)}, s32[8]{0:T(128)}, u32[]{:S(2)}) copy-start(s32[8]{0:T(128)} %param.37) | copy-start | bytes 100
  70.0 19.7 %all-to-all-start = ((bf16[8,256,256]{2,1,0:T(8,128)(2,1)}), bf16[8,256,256]{2,1,0:T(8,128)(2,1)}, u32[]{:S(2)}, u32[]{:S(2)}) async-start(bf16[8,256,256]{2,1,0:T(8,128)(2,1)} %bitcast.52), calls=%async_computation.1 | async-start | bytes 2097152 | tf_op jit(solution)/shard_map/all_to_all | solution.py:150
  92.5 7.0 %copy-start.9 = (bf16[64,2048]{1,0:T(8,128)(2,1)S(1)}, bf16[64,2048]{1,0:T(8,128)(2,1)}, u32[]{:S(2)}) copy-start(bf16[64,2048]{1,0:T(8,128)(2,1)} %param.29) | copy-start | bytes 786436
  94.9 21.0 %copy-start.10 = (bf16[128,256]{1,0:T(8,128)(2,1)S(1)}, bf16[128,256]{1,0:T(8,128)(2,1)}, u32[]{:S(2)}) copy-start(bf16[128,256]{1,0:T(8,128)(2,1)} %param.20) | copy-start | bytes 196612
  94.9 21.1 %copy-start.11 = (f32[2048]{0:T(1024)S(1)}, f32[2048]{0:T(1024)}, u32[]{:S(2)}) copy-start(f32[2048]{0:T(1024)} %param.30) | copy-start | bytes 24580
  94.9 21.1 %copy-start.12 = (f32[2048]{0:T(1024)S(1)}, f32[2048]{0:T(1024)}, u32[]{:S(2)}) copy-start(f32[2048]{0:T(1024)} %param.27) | copy-start | bytes 24580
  94.9 19.8 %all-to-all-start.1 = ((bf16[8,256,256]{2,1,0:T(8,128)(2,1)}), bf16[8,256,256]{2,1,0:T(8,128)(2,1)}, u32[]{:S(2)}, u32[]{:S(2)}) async-start(bf16[8,256,256]{2,1,0:T(8,128)(2,1)} %broadcast_select_fusion.1), calls=%async_computation.2 | async-start | bytes 2097152 | tf_op jit(solution)/shard_map/all_to_all | solution.py:161
  115.9 4.3 %copy-start.14 = (f32[2048]{0:T(1024)S(1)}, f32[2048]{0:T(1024)}, u32[]{:S(2)}) copy-start(f32[2048]{0:T(1024)} %param.33) | copy-start | bytes 24580
Sparse Core Ops, SparseCore 0:
  17.2 30.6 all-gather.2
  64.8 43.3 reduce-scatter.1
where the time goes:
time: 133 us
  waiting for transfers between devices  35.2 us (26%)
  matrix products  26.4 us (20%)
  other arithmetic  24.5 us (18%)
  local copies, waits for them, and re-layouts  22.2 us (17%)
  between operations  15.3 us (12%)
  starting transfers between devices  9.1 us (7%)
    all_to_all x1, waiting for transfers between devices, on_device(): lax.all_to_all(full_seq.reshape(blocks, block_span, head_dim), 'blk', spl...  14.7 us
    all_to_all x1, waiting for transfers between devices, on_device(): lax.all_to_all(arranged, 'blk', split_axis=0, concat_axis=0, tiled=True)  12.3 us
    all_gather x1, waiting for transfers between devices, on_device(): gathered = lax.all_gather(fresh_slot[None], 'head', axis=0, tiled=True)  8.1 us
    dot_general x2, matrix products, scores_of(): lax.dot_general(rows, keys, (((1,), (1,)), ((), ())), preferred_element_t...  5.25 us
    unnamed x43, local copies, waits for them, and re-layouts  4.89 us
    all_to_all x1, starting transfers between devices, on_device(): lax.all_to_all(arranged, 'blk', split_axis=0, concat_axis=0, tiled=True)  4.6 us
    reduce_sum x2, other arithmetic, on_device(): row_total = jnp.sum(old_exp, axis=1) + jnp.sum(new_exp, axis=1)  4.57 us
    dot_general x1, matrix products, on_device(): jnp.dot(normed, w_query, preferred_element_type=jnp.float32)  4.49 us
  transfers between devices with their start and end apart: 4, of which 3 were waited for; matrix products, arithmetic and copies ran while one was open for 27% of the time, Pallas kernels for 0%

commit v1 on v0

v1 whole, which is shorter than its diff:
```python
import functools

import jax
import jax.numpy as jnp
from jax import lax
from jax.experimental import pallas as pl
from jax.experimental.pallas import tpu as pltpu
from jax.sharding import PartitionSpec as P

QH = 8

eps = 1e-06
rope_base = 1000000.0
VMEM_BYTES = 40 * 1024 * 1024


def rms_scale(values):
    return values * lax.rsqrt(jnp.mean(values * values, axis=-1, keepdims=True) + eps)


def rotate(values, cosine, sine):
    half_dim = values.shape[-1] // 2
    lower = values[:, :half_dim]
    upper = values[:, half_dim:]
    return jnp.concatenate([lower * cosine - upper * sine, upper * cosine + lower * sine], axis=-1)


def matmul(rows, columns):
    return jnp.dot(rows, columns, preferred_element_type=jnp.float32)


def scores_of(rows, keys):
    return lax.dot_general(rows, keys, (((1,), (1,)), ((), ())), preferred_element_type=jnp.float32)


def call(body, out_shape, grid, in_specs, out_specs, scalars, operands, flops, moved, scratch=()):
    return pl.pallas_call(
        body,
        out_shape=out_shape,
        grid_spec=pltpu.PrefetchScalarGridSpec(
            num_scalar_prefetch=len(scalars),
            grid=grid,
            in_specs=in_specs,
            out_specs=out_specs,
            scratch_shapes=list(scratch),
        ),
        compiler_params=pltpu.CompilerParams(vmem_limit_bytes=VMEM_BYTES),
        cost_estimate=pl.CostEstimate(flops=flops, bytes_accessed=moved, transcendentals=0),
    )(*scalars, *operands)


def whole(shape):
    return pl.BlockSpec(shape, lambda *_: (0,) * len(shape))


def project_body(is_key, hidden, in_gain, w_query, w_keyval, q_gain, k_gain, cosine, sine, q_out, fresh_out):
    heads, _, head_dim = q_out.shape
    normed = (rms_scale(hidden[...].astype(jnp.float32)) * in_gain[...]).astype(jnp.bfloat16)
    cos, sin = cosine[...], sine[...]
    own = rms_scale(matmul(normed, w_keyval[...]))
    turned = rotate(own * k_gain[...], cos, sin)
    fresh_out[...] = jnp.where(is_key[0] > 0, turned, own).astype(jnp.bfloat16)
    queries = matmul(normed, w_query[...])
    for h in range(heads):
        part = queries[:, h * head_dim : (h + 1) * head_dim]
        q_out[h] = rotate(rms_scale(part) * q_gain[...], cos, sin).astype(jnp.bfloat16)


def sequence_body(table, place, fresh, pool, out, pages, wide, sems):
    n_pages = sems.shape[0]
    page_len = pool.shape[2]
    length = place[0]
    slot = place[1]
    copies = [
        pltpu.make_async_copy(
            pool.at[table[j], slot], pages.at[pl.ds(j * page_len, page_len)], sems.at[j]
        )
        for j in range(n_pages)
    ]
    for c in copies:
        c.start()
    prefix = n_pages * page_len
    rows = fresh.shape[0]
    wide[...] = jnp.zeros_like(wide)
    base = pl.multiple_of(lax.div(length, 8) * 8, 8)
    padded = jnp.concatenate([fresh[...].astype(jnp.float32), jnp.zeros((8, wide.shape[1]), jnp.float32)], axis=0)
    wide[pl.ds(base, rows + 8), :] = pltpu.roll(padded, lax.rem(length, 8), 0)
    for c in copies:
        c.wait()
    at = lax.broadcasted_iota(jnp.int32, (prefix, 1), 0)
    old = pages[...].astype(jnp.float32)
    out[:prefix, :] = jnp.where(at < length, old, wide[:prefix, :]).astype(jnp.bfloat16)
    out[prefix:, :] = wide[prefix : prefix + rows, :].astype(jnp.bfloat16)


def arrange_body(owner, spread, out, sems):
    n = spread.shape[0]

    def start(r, carry):
        pltpu.make_async_copy(spread.at[r], out.at[owner[r]], sems.at[r]).start()
        return carry

    def wait(r, carry):
        pltpu.make_async_copy(spread.at[r], out.at[owner[r]], sems.at[r]).wait()
        return carry

    lax.fori_loop(0, n, start, 0)
    lax.fori_loop(0, n, wait, 0)


def old_body(table, place, queries, pool, acc_out, top_out, total_out, keys, values, sems):
    n_pages = sems.shape[1]
    page_len = pool.shape[2]
    length = place[0]
    key_slot = place[1]
    value_slot = place[2]

    @pl.when(pl.program_id(0) == 0)
    def _():
        copies = []
        for j in range(n_pages):
            at = pl.ds(j * page_len, page_len)
            copies.append(pltpu.make_async_copy(pool.at[table[j], key_slot], keys.at[at], sems.at[0, j]))
        for j in range(n_pages):
            at = pl.ds(j * page_len, page_len)
            copies.append(pltpu.make_async_copy(pool.at[table[j], value_slot], values.at[at], sems.at[1, j]))
        for c in copies:
            c.start()
        for c in copies:
            c.wait()

    scores = scores_of(queries[...], keys[...])
    at = lax.broadcasted_iota(jnp.int32, (1, scores.shape[1]), 1)
    scores = jnp.where(at < length, scores, -jnp.inf)
    top = jnp.max(scores, axis=1, keepdims=True)
    expo = jnp.exp(scores - top)
    top_out[...] = top
    total_out[...] = jnp.sum(expo, axis=1, keepdims=True)
    acc_out[...] = matmul(expo.astype(jnp.bfloat16), values[...])


def new_body(place, queries, key, value, acc, top_in, total_in, w_out, part_out):
    heads, rows, head_dim = queries.shape
    new_rows = key.shape[1]
    row_at = lax.broadcasted_iota(jnp.int32, (rows, new_rows), 0) + pl.program_id(0) * rows
    causal = lax.broadcasted_iota(jnp.int32, (rows, new_rows), 1) <= row_at
    sides = []
    for h in range(heads):
        scores = jnp.where(causal, scores_of(queries[h], key[0]), -jnp.inf)
        top_old = top_in[h]
        top = jnp.maximum(top_old, jnp.max(scores, axis=1, keepdims=True))
        expo = jnp.exp(scores - top)
        scale = jnp.exp(top_old - top)
        total = total_in[h] * scale + jnp.sum(expo, axis=1, keepdims=True)
        mix = acc[h] * scale + matmul(expo.astype(jnp.bfloat16), value[0])
        sides.append((mix / total).astype(jnp.bfloat16))
    attn = jnp.concatenate(sides, axis=1)
    part_out[...] = matmul(attn, w_out[...]).astype(jnp.bfloat16)


def base_body(place, hidden, in_gain, left, right, laurel_gain, base_out):
    tokens = hidden[...].astype(jnp.float32)
    normed = (rms_scale(tokens) * in_gain[...]).astype(jnp.bfloat16)
    low = matmul(normed, left[...]).astype(jnp.bfloat16)
    laurel = normed.astype(jnp.float32) + rms_scale(matmul(low, right[...])) * laurel_gain[...]
    base_out[...] = tokens + laurel


def tail_body(base, proj, post_gain, layer_input, w_plgate, w_plproj, pl_gain, out):
    state = (base[...] + rms_scale(proj[...].astype(jnp.float32)) * post_gain[...]) * 2.0 ** (-0.5)
    gate = jax.nn.gelu(matmul(state.astype(jnp.bfloat16), w_plgate[...]), approximate=True)
    gated = (gate * layer_input[...].astype(jnp.float32)).astype(jnp.bfloat16)
    out[...] = (state + rms_scale(matmul(gated, w_plproj[...])) * pl_gain[...]).astype(jnp.bfloat16)


def on_device(
    hidden_in,
    layer_input,
    in_gain,
    w_query,
    w_keyval,
    q_gain,
    k_gain,
    w_out,
    post_gain,
    laurel_left,
    laurel_right,
    laurel_gain,
    w_plgate,
    w_plproj,
    pl_gain,
    kv_pool,
    page_table,
    prefix_len,
    decode_owner,
):
    new_rows, width = hidden_in.shape
    head_dim = kv_pool.shape[3]
    page_len = kv_pool.shape[2]
    n_pages = page_table.shape[1]
    kv_heads = kv_pool.shape[1] // 2
    local_heads = w_query.shape[1] // head_dim
    prefix_max = n_pages * page_len
    total_len = prefix_max + new_rows
    blocks = lax.axis_size("blk")
    block_span = total_len // blocks
    head_idx = lax.axis_index("head").astype(jnp.int32)
    kv_of = head_idx * local_heads // (QH // kv_heads)
    length = prefix_len[0]
    table = page_table[0]
    bf16, f32 = jnp.bfloat16, jnp.float32
    in_hbm = pl.BlockSpec(memory_space=pl.ANY)
    half_dim = head_dim // 2
    row = lambda v: v.reshape(1, -1)

    positions = length + jnp.arange(new_rows, dtype=jnp.int32)
    frequency = rope_base ** (-jnp.arange(half_dim, dtype=jnp.float32) / half_dim)
    angles = positions.astype(jnp.float32)[:, None] * frequency[None, :]
    cosine, sine = jnp.cos(angles), jnp.sin(angles)

    tile = new_rows // 2
    rows_of = lambda cols: pl.BlockSpec((tile, cols), lambda i, *_: (i, 0))
    queries, fresh = call(
        project_body,
        (
            jax.ShapeDtypeStruct((local_heads, new_rows, head_dim), bf16),
            jax.ShapeDtypeStruct((new_rows, head_dim), bf16),
        ),
        (new_rows // tile,),
        [
            rows_of(width),
            whole((1, width)),
            whole(w_query.shape),
            whole(w_keyval.shape),
            whole((1, head_dim)),
            whole((1, head_dim)),
            rows_of(half_dim),
            rows_of(half_dim),
        ],
        (
            pl.BlockSpec((local_heads, tile, head_dim), lambda i, *_: (0, i, 0)),
            rows_of(head_dim),
        ),
        [(head_idx < kv_heads).astype(jnp.int32).reshape(1)],
        [hidden_in, row(in_gain), w_query, w_keyval, row(q_gain), row(k_gain), cosine, sine],
        2 * new_rows * width * (local_heads + 1) * head_dim,
        8 << 20,
    )

    gathered = lax.all_gather(fresh[None], "head", axis=0, tiled=True)

    full_seq = call(
        sequence_body,
        jax.ShapeDtypeStruct((total_len, head_dim), bf16),
        (1,),
        [whole((new_rows, head_dim)), in_hbm],
        whole((total_len, head_dim)),
        [table, jnp.stack([length, head_idx])],
        [fresh, kv_pool],
        1 << 20,
        4 << 20,
        [
            pltpu.VMEM((prefix_max, head_dim), bf16),
            pltpu.VMEM((total_len + 8, head_dim), f32),
            pltpu.SemaphoreType.DMA((n_pages,)),
        ],
    )
    spread = lax.all_to_all(
        full_seq.reshape(blocks, block_span, head_dim), "blk", split_axis=0, concat_axis=0, tiled=True
    )

    place = jnp.stack([length, kv_of, kv_of + kv_heads])
    flat = local_heads * new_rows
    q_tile = flat // 4
    q_rows = lambda cols: pl.BlockSpec((q_tile, cols), lambda i, *_: (i, 0))
    acc, top, total = call(
        old_body,
        (
            jax.ShapeDtypeStruct((flat, head_dim), f32),
            jax.ShapeDtypeStruct((flat, 1), f32),
            jax.ShapeDtypeStruct((flat, 1), f32),
        ),
        (flat // q_tile,),
        [q_rows(head_dim), in_hbm],
        (q_rows(head_dim), q_rows(1), q_rows(1)),
        [table, place],
        [queries.reshape(flat, head_dim), kv_pool],
        8 * flat * prefix_max * head_dim,
        8 << 20,
        [
            pltpu.VMEM((prefix_max, head_dim), bf16),
            pltpu.VMEM((prefix_max, head_dim), bf16),
            pltpu.SemaphoreType.DMA((2, n_pages)),
        ],
    )

    heads_of = lambda cols: pl.BlockSpec((local_heads, tile, cols), lambda i, *_: (0, i, 0))
    part = call(
        new_body,
        jax.ShapeDtypeStruct((new_rows, width), bf16),
        (new_rows // tile,),
        [
            heads_of(head_dim),
            pl.BlockSpec((1, new_rows, head_dim), lambda i, p: (p[1], 0, 0)),
            pl.BlockSpec((1, new_rows, head_dim), lambda i, p: (p[2], 0, 0)),
            heads_of(head_dim),
            heads_of(1),
            heads_of(1),
            whole(w_out.shape),
        ],
        rows_of(width),
        [place],
        [
            queries,
            gathered,
            gathered,
            acc.reshape(local_heads, new_rows, head_dim),
            top.reshape(local_heads, new_rows, 1),
            total.reshape(local_heads, new_rows, 1),
            w_out,
        ],
        8 * flat * new_rows * head_dim,
        8 << 20,
    )
    proj_rows = lax.psum_scatter(part, "head", scatter_dimension=0, tiled=True)

    quarter = new_rows // lax.axis_size("head")
    rank = laurel_left.shape[1]
    gate_dim = w_plgate.shape[1]
    base = call(
        base_body,
        jax.ShapeDtypeStruct((quarter, width), f32),
        (1,),
        [
            pl.BlockSpec((quarter, width), lambda i, p: (p[0], 0)),
            whole((1, width)),
            whole((width, rank)),
            whole((rank, width)),
            whole((1, width)),
        ],
        whole((quarter, width)),
        [head_idx.reshape(1)],
        [hidden_in, row(in_gain), laurel_left, laurel_right, row(laurel_gain)],
        1 << 28,
        4 << 20,
    )

    arranged = call(
        arrange_body,
        jax.ShapeDtypeStruct(spread.shape, bf16),
        (1,),
        [in_hbm],
        in_hbm,
        [decode_owner],
        [spread],
        1 << 10,
        2 << 20,
        [pltpu.SemaphoreType.DMA((blocks,))],
    )
    owned = lax.all_to_all(arranged, "blk", split_axis=0, concat_axis=0, tiled=True)

    mixed = call(
        tail_body,
        jax.ShapeDtypeStruct((quarter, width), bf16),
        (1,),
        [
            whole((quarter, width)),
            whole((quarter, width)),
            whole((1, width)),
            whole((quarter, gate_dim)),
            whole(w_plgate.shape),
            whole(w_plproj.shape),
            whole((1, width)),
        ],
        whole((quarter, width)),
        [],
        [base, proj_rows, row(post_gain), layer_input, w_plgate, w_plproj, row(pl_gain)],
        1 << 28,
        6 << 20,
    )
    return (mixed, owned.reshape(1, 1, total_len, head_dim))


def solution(mesh):
    in_specs = (
        P("blk", None),
        P(("blk", "head"), None),
        P(),
        P(None, "head"),
        P(None, "head"),
        P(),
        P(),
        P("head", None),
        P(),
        P(),
        P(),
        P(),
        P(),
        P(),
        P(),
        P("blk", None, None, None),
        P("blk", None),
        P("blk"),
        P(),
    )
    out_specs = (P(("blk", "head"), None), P("head", "blk", None, None))
    return jax.shard_map(
        on_device, mesh=mesh, in_specs=in_specs, out_specs=out_specs, check_vma=False
    )
```

time: 133 us -> 120 us (0.902)
  matrix products: 26.4 us -> 0 us
  Pallas kernels: 0 us -> 24 us
  other arithmetic: 24.5 us -> 1.15 us
  blocking collectives: 0 us -> 18.8 us
  starting transfers between devices: 9.1 us -> 4.34 us
  waiting for transfers between devices: 35.2 us -> 31.7 us
  local copies, waits for them, and re-layouts: 22.2 us -> 24.5 us
    dot_general x9 -> x0, matrix products: 26.4 us -> none  [the longest x2 5.25 us: scores_of(): lax.dot_general(rows, keys, (((1,), (1,)), ((), ())), preferred_element_t...]
    pallas_call x0 -> x7, Pallas kernels: none -> 24 us  [call(): pl.pallas_call(body, out_shape=out_shape, grid_spec=pltpu.PrefetchScalarG...]
    unnamed x43 -> x64, local copies, waits for them, and re-layouts: 4.89 us -> 24.5 us
    all_to_all x0 -> x1, blocking collectives: none -> 18.8 us  [on_device(): lax.all_to_all(full_seq.reshape(blocks, block_span, head_dim), 'blk', spl...]
    all_to_all x1 -> x0, waiting for transfers between devices: 14.7 us -> none  [on_device(): lax.all_to_all(full_seq.reshape(blocks, block_span, head_dim), 'blk', spl...]
    all_gather x1, waiting for transfers between devices: 8.1 us -> 19.1 us  [on_device(): gathered = lax.all_gather(fresh[None], 'head', axis=0, tiled=True)]
    reduce_sum x4 -> x0, other arithmetic: 8.02 us -> none  [the longest x2 4.57 us: on_device(): row_total = jnp.sum(old_exp, axis=1) + jnp.sum(new_exp, axis=1)]
    select_n x6 -> x0, other arithmetic: 7.87 us -> none  [the longest x2 4.01 us: on_device(): my_pages = jnp.take(kv_pool, page_table[0], axis=0)]
  transfers between devices with their start and end apart: 4 -> 3, of which waited for: 3 -> 3; matrix products, arithmetic and copies ran while one was open for 27% -> 0% of each run, Pallas kernels for 0% -> 11%
where the time goes in v1:
time: 120 us; the launch traced here: 119 us
  waiting for transfers between devices  31.7 us (26%)
  local copies, waits for them, and re-layouts  24.5 us (20%)
  Pallas kernels  24 us (20%)
  blocking collectives  18.8 us (16%)
  between operations  14.9 us (12%)
  starting transfers between devices  4.34 us (4%)
    unnamed x64, local copies, waits for them, and re-layouts  24.5 us
    pallas_call x7, Pallas kernels, call(): pl.pallas_call(body, out_shape=out_shape, grid_spec=pltpu.PrefetchScalarG...  24 us
    all_gather x1, waiting for transfers between devices, on_device(): gathered = lax.all_gather(fresh[None], 'head', axis=0, tiled=True)  19.1 us
    all_to_all x1, blocking collectives, on_device(): lax.all_to_all(full_seq.reshape(blocks, block_span, head_dim), 'blk', spl...  18.8 us
    all_to_all x1, waiting for transfers between devices, on_device(): lax.all_to_all(arranged, 'blk', split_axis=0, concat_axis=0, tiled=True)  12.5 us
    all_to_all x1, starting transfers between devices, on_device(): lax.all_to_all(arranged, 'blk', split_axis=0, concat_axis=0, tiled=True)  4.26 us
  transfers between devices with their start and end apart: 3, of which 3 were waited for; matrix products, arithmetic and copies ran while one was open for 0% of the time, Pallas kernels for 11%

profile of v1, /device:TPU:0, one launch (start us, length us, event | category | flops | bytes accessed | tf_op | source)
XLA Modules:
  0.0 119.4 jit_solution(6212719252192311490)
XLA Ops:
  8.9 1.6 %copy-done.3 = bf16[512,2048]{1,0:T(8,128)(2,1)S(1)} copy-done((bf16[512,2048]{1,0:T(8,128)(2,1)S(1)}, bf16[512,2048]{1,0:T(8,128)(2,1)}, u32[]{:S(2)}) %copy-start.3) | copy-done | bytes 2097176
  11.2 1.6 %copy-done.26 = bf16[2048,512]{1,0:T(8,128)(2,1)S(1)} copy-done((bf16[2048,512]{1,0:T(8,128)(2,1)S(1)}, bf16[2048,512]{1,0:T(8,128)(2,1)}, u32[]{:S(2)}) %copy-start.26) | copy-done | bytes 2097176
  12.8 1.2 %copy-done.27 = bf16[2048,256]{1,0:T(8,128)(2,1)S(1)} copy-done((bf16[2048,256]{1,0:T(8,128)(2,1)S(1)}, bf16[2048,256]{1,0:T(8,128)(2,1)}, u32[]{:S(2)}) %copy-start.27) | copy-done | bytes 1048600
  15.4 3.5 %shard_map.195 = (bf16[2,512,256]{2,1,0:T(8,128)(2,1)S(1)}, bf16[512,256]{1,0:T(8,128)(2,1)}) custom-call(s32[1]{0:T(128)} %bitcast.5.is_key, bf16[512,2048]{1,0:T(8,128)(2,1)S(1)} %copy-done.3, f32[1,2048]{1,0:T(1,128)S(1)} %bitcast.27, bf16[2048,512]{1,0:T(8,128)(2,1)S(1)} %copy-done.26, bf16[2048,256]{1,0:T(8,128)(2,1)S(1)} %copy-done.27, ...), custom_call_target="tpu_custom_call" | custom-call | flops 1610612736 | bytes 8388608 | tf_op jit(solution)/shard_map/pallas_call | solution.py:37
  19.8 1.0 copy-done.10
  20.9 8.0 %shard_map.196 = (f32[1024,256]{1,0:T(8,128)S(1)}, f32[1024,1]{1,0:T(8,128)S(1)}, f32[1024,1]{1,0:T(8,128)S(1)}) custom-call(s32[12]{0:T(128)S(1)} %bitcast.32, s32[3]{0:T(128)S(1)} %pad_add_fusion.place, bf16[1024,256]{1,0:T(8,128)(2,1)S(1)} %bitcast.24, bf16[12,4,128,256]{3,2,1,0:T(8,128)(2,1)S(1)} %copy-done.1), custom_call_target="tpu_custom_call" | custom-call | flops 3221225472 | bytes 8388608 | tf_op jit(solution)/shard_map/pallas_call | solution.py:37
  31.4 19.1 %all-gather.3.cloned.1.call-done = bf16[2048,256]{1,0:T(8,128)(2,1)} async-done(((bf16[512,256]{1,0:T(8,128)(2,1)}), bf16[2048,256]{1,0:T(8,128)(2,1)}) %all-gather.3.cloned.1.call-update) | async-done | bytes 1048592 | tf_op jit(solution)/shard_map/all_gather | solution.py:250
  50.5 1.2 %copy-done = bf16[2048,256]{1,0:T(8,128)(2,1)S(1)} copy-done((bf16[2048,256]{1,0:T(8,128)(2,1)S(1)}, bf16[2048,256]{1,0:T(8,128)(2,1)}, u32[]{:S(2)}) %copy-start) | copy-done | bytes 1048600
  51.7 1.6 %copy-done.2 = bf16[512,2048]{1,0:T(8,128)(2,1)S(1)} copy-done((bf16[512,2048]{1,0:T(8,128)(2,1)S(1)}, bf16[512,2048]{1,0:T(8,128)(2,1)}, u32[]{:S(2)}) %copy-start.2) | copy-done | bytes 2097176
  53.3 1.2 %copy-done.6 = f32[1024,256]{1,0:T(8,128)S(1)} copy-done((f32[1024,256]{1,0:T(8,128)S(1)}, f32[1024,256]{1,0:T(8,128)}, u32[]{:S(2)}) %copy-start.6) | copy-done | bytes 1048600
  54.5 1.0 copy-done.11
  55.6 1.0 copy-done.13
  56.6 1.0 copy-done.15
  57.7 4.9 %shard_map.197 = bf16[512,2048]{1,0:T(8,128)(2,1)} custom-call(s32[3]{0:T(128)S(1)} %pad_add_fusion.place, bf16[2,512,256]{2,1,0:T(8,128)(2,1)S(1)} %copy-done.11, bf16[4,512,256]{2,1,0:T(8,128)(2,1)S(1)} %bitcast.20, bf16[4,512,256]{2,1,0:T(8,128)(2,1)S(1)} %bitcast.21, f32[2,512,256]{2,1,0:T(8,128)S(1)} %bitcast.23, f32[2,512,1]{2,1,0:T(8,128)S(1)} %bitcast.25, ...), custom_call_target="tpu_custom_call" | custom-call | flops 1073741824 | bytes 8388608 | tf_op jit(solution)/shard_map/pallas_call | solution.py:37
  62.6 3.2 %shard_map.199 = bf16[2048,256]{1,0:T(8,128)(2,1)S(1)} custom-call(s32[12]{0:T(128)S(1)} %bitcast.33, s32[2]{0:T(128)S(1)} %pad_add_fusion.1.place, bf16[512,256]{1,0:T(8,128)(2,1)} %get-tuple-element.8.fresh, bf16[12,4,128,256]{3,2,1,0:T(8,128)(2,1)S(1)} %copy-done.1), custom_call_target="tpu_custom_call" | custom-call | flops 1048576 | bytes 4194304 | tf_op jit(solution)/shard_map/pallas_call | solution.py:37
  65.9 18.8 %all_to_all.10.spread = bf16[8,256,256]{2,1,0:T(8,128)(2,1)S(1)} all-to-all(bf16[8,256,256]{2,1,0:T(8,128)(2,1)S(1)} %bitcast.22), channel_id=1, replica_groups=mesh['blk'=8,'head'=4] {'blk'}, dimensions={0} | all-to-all | bytes 2097152 | tf_op jit(solution)/shard_map/all_to_all | solution.py:268
  84.7 1.6 %shard_map.200 = bf16[8,256,256]{2,1,0:T(8,128)(2,1)} custom-call(s32[8]{0:T(128)S(1)} %copy-done.25, bf16[8,256,256]{2,1,0:T(8,128)(2,1)S(1)} %all_to_all.10.spread), custom_call_target="tpu_custom_call" | custom-call | flops 1024 | bytes 2097152 | tf_op jit(solution)/shard_map/pallas_call | solution.py:37
  86.3 4.3 %all-to-all-start.1 = ((bf16[8,256,256]{2,1,0:T(8,128)(2,1)}), bf16[8,256,256]{2,1,0:T(8,128)(2,1)}, u32[]{:S(2)}, u32[]{:S(2)}) async-start(bf16[8,256,256]{2,1,0:T(8,128)(2,1)} %shard_map.200), calls=%async_computation.2 | async-start | bytes 2097152 | tf_op jit(solution)/shard_map/all_to_all | solution.py:360
  90.9 1.6 %copy-done.4 = bf16[512,2048]{1,0:T(8,128)(2,1)S(1)} copy-done((bf16[512,2048]{1,0:T(8,128)(2,1)S(1)}, bf16[512,2048]{1,0:T(8,128)(2,1)}, u32[]{:S(2)}) %copy-start.4) | copy-done | bytes 2097176
  93.4 12.5 %all-to-all-done.1 = bf16[8,256,256]{2,1,0:T(8,128)(2,1)} async-done(((bf16[8,256,256]{2,1,0:T(8,128)(2,1)}), bf16[8,256,256]{2,1,0:T(8,128)(2,1)}, u32[]{:S(2)}, u32[]{:S(2)}) %all-to-all-start.1) | async-done | bytes 1048608 | tf_op jit(solution)/shard_map/all_to_all | solution.py:360
  106.1 1.2 %copy-done.8 = bf16[256,2048]{1,0:T(8,128)(2,1)S(1)} copy-done((bf16[256,2048]{1,0:T(8,128)(2,1)S(1)}, bf16[256,2048]{1,0:T(8,128)(2,1)}, u32[]{:S(2)}) %copy-start.8) | copy-done | bytes 1048600
  107.3 1.0 copy-done.16
  108.3 2.0 %shard_map.198 = bf16[128,2048]{1,0:T(8,128)(2,1)} custom-call(f32[128,2048]{1,0:T(8,128)S(1)} %shard_map.194.base, bf16[128,2048]{1,0:T(8,128)(2,1)S(1)} %copy-done.16, f32[1,2048]{1,0:T(1,128)S(1)} %bitcast.30, bf16[128,256]{1,0:T(8,128)(2,1)S(1)} %copy-done.18, bf16[2048,256]{1,0:T(8,128)(2,1)S(1)} %copy-done.7, bf16[256,2048]{1,0:T(8,128)(2,1)S(1)} %copy-done.8, ...), custom_call_target="tpu_custom_call" | custom-call | flops 268435456 | bytes 6291456 | tf_op jit(solution)/shard_map/pallas_call | solution.py:37
  110.3 2.3 %copy.24 = bf16[1,1,2048,256]{3,2,1,0:T(8,128)(2,1)} copy(bf16[1,1,2048,256]{3,2,1,0:T(8,128)(2,1)} %bitcast.18) | data formatting | bytes 2097152
  (61 shorter events, 8.1 us)
Async XLA Ops:
  7.2 43.3 %all-gather.3.cloned.1.call-start = ((), (), s32[]{:S(2)}) async-start(), calls=%async_computation.4 | async-start | bytes 1310720 | tf_op jit(solution)/shard_map/all_gather | solution.py:250
  8.9 1.6 %copy-start.3 = (bf16[512,2048]{1,0:T(8,128)(2,1)S(1)}, bf16[512,2048]{1,0:T(8,128)(2,1)}, u32[]{:S(2)}) copy-start(bf16[512,2048]{1,0:T(8,128)(2,1)} %hidden.3) | copy-start | bytes 6291460
  11.2 1.6 %copy-start.26 = (bf16[2048,512]{1,0:T(8,128)(2,1)S(1)}, bf16[2048,512]{1,0:T(8,128)(2,1)}, u32[]{:S(2)}) copy-start(bf16[2048,512]{1,0:T(8,128)(2,1)} %w_query.1) | copy-start | bytes 6291460
  12.8 1.2 %copy-start.27 = (bf16[2048,256]{1,0:T(8,128)(2,1)S(1)}, bf16[2048,256]{1,0:T(8,128)(2,1)}, u32[]{:S(2)}) copy-start(bf16[2048,256]{1,0:T(8,128)(2,1)} %w_keyval.1) | copy-start | bytes 3145732
  15.4 4.5 %copy-start.1 = (bf16[12,4,128,256]{3,2,1,0:T(8,128)(2,1)S(1)}, bf16[12,4,128,256]{3,2,1,0:T(8,128)(2,1)}, u32[]{:S(2)}) copy-start(bf16[12,4,128,256]{3,2,1,0:T(8,128)(2,1)} %pool.3) | copy-start | bytes 9437188
  15.4 4.5 %copy-start.24 = (s32[1,12]{1,0:T(1,128)S(1)}, s32[1,12]{1,0:T(1,128)}, u32[]{:S(2)}) copy-start(s32[1,12]{1,0:T(1,128)} %param.35) | copy-start | bytes 148
  19.7 86.4 %reduce-scatter.2.cloned.1.call-start = ((), (), s32[]{:S(2)}) async-start(), calls=%async_computation.3 | async-start | bytes 2621440 | tf_op jit(solution)/shard_map/reduce_scatter | solution.py:325
  19.8 1.0 copy-start.10
  50.5 1.2 %copy-start = (bf16[2048,256]{1,0:T(8,128)(2,1)S(1)}, bf16[2048,256]{1,0:T(8,128)(2,1)}, u32[]{:S(2)}) copy-start(bf16[2048,256]{1,0:T(8,128)(2,1)} %all-gather.3.cloned.1.call-done) | copy-start | bytes 3145732
  51.7 1.6 %copy-start.2 = (bf16[512,2048]{1,0:T(8,128)(2,1)S(1)}, bf16[512,2048]{1,0:T(8,128)(2,1)}, u32[]{:S(2)}) copy-start(bf16[512,2048]{1,0:T(8,128)(2,1)} %w_out.1) | copy-start | bytes 6291460
  53.3 1.2 %copy-start.6 = (f32[1024,256]{1,0:T(8,128)S(1)}, f32[1024,256]{1,0:T(8,128)}, u32[]{:S(2)}) copy-start(f32[1024,256]{1,0:T(8,128)} %copy-done.5) | copy-start | bytes 3145732
  54.5 1.0 copy-start.11
  65.8 18.8 %copy-start.25 = (s32[8]{0:T(128)S(1)}, s32[8]{0:T(128)}, u32[]{:S(2)}) copy-start(s32[8]{0:T(128)} %owner.1) | copy-start | bytes 100
  84.7 5.9 %copy-start.30 = (bf16[2048,64]{0,1:T(8,128)(2,1)S(1)}, bf16[2048,64]{0,1:T(8,128)(2,1)}, u32[]{:S(2)}) copy-start(bf16[2048,64]{0,1:T(8,128)(2,1)} %param.28) | copy-start | bytes 786436
  84.7 6.2 %copy-start.17 = (bf16[64,2048]{1,0:T(8,128)(2,1)S(1)}, bf16[64,2048]{1,0:T(8,128)(2,1)}, u32[]{:S(2)}) copy-start(bf16[64,2048]{1,0:T(8,128)(2,1)} %right.1) | copy-start | bytes 786436
  84.7 6.2 %copy-start.20 = (f32[2048]{0:T(1024)S(1)}, f32[2048]{0:T(1024)}, u32[]{:S(2)}) copy-start(f32[2048]{0:T(1024)} %param.21) | copy-start | bytes 24580
  84.7 6.2 %copy-start.21 = (f32[2048]{0:T(1024)S(1)}, f32[2048]{0:T(1024)}, u32[]{:S(2)}) copy-start(f32[2048]{0:T(1024)} %param.30) | copy-start | bytes 24580
  86.3 19.7 %all-to-all-start.1 = ((bf16[8,256,256]{2,1,0:T(8,128)(2,1)}), bf16[8,256,256]{2,1,0:T(8,128)(2,1)}, u32[]{:S(2)}, u32[]{:S(2)}) async-start(bf16[8,256,256]{2,1,0:T(8,128)(2,1)} %shard_map.200), calls=%async_computation.2 | async-start | bytes 2097152 | tf_op jit(solution)/shard_map/all_to_all | solution.py:360
  90.9 1.6 %copy-start.4 = (bf16[512,2048]{1,0:T(8,128)(2,1)S(1)}, bf16[512,2048]{1,0:T(8,128)(2,1)}, u32[]{:S(2)}) copy-start(bf16[512,2048]{1,0:T(8,128)(2,1)} %hidden.3) | copy-start | bytes 6291460
  92.5 13.6 %copy-start.7 = (bf16[2048,256]{1,0:T(8,128)(2,1)S(1)}, bf16[2048,256]{1,0:T(8,128)(2,1)}, u32[]{:S(2)}) copy-start(bf16[2048,256]{1,0:T(8,128)(2,1)} %w_plgate.1) | copy-start | bytes 3145732
  92.5 13.6 %copy-start.18 = (bf16[128,256]{1,0:T(8,128)(2,1)S(1)}, bf16[128,256]{1,0:T(8,128)(2,1)}, u32[]{:S(2)}) copy-start(bf16[128,256]{1,0:T(8,128)(2,1)} %layer_input.1) | copy-start | bytes 196612
  92.5 13.6 %copy-start.22 = (f32[2048]{0:T(1024)S(1)}, f32[2048]{0:T(1024)}, u32[]{:S(2)}) copy-start(f32[2048]{0:T(1024)} %param.27) | copy-start | bytes 24580
  92.5 13.6 %copy-start.23 = (f32[2048]{0:T(1024)S(1)}, f32[2048]{0:T(1024)}, u32[]{:S(2)}) copy-start(f32[2048]{0:T(1024)} %param.33) | copy-start | bytes 24580
  106.1 1.2 %copy-start.8 = (bf16[256,2048]{1,0:T(8,128)(2,1)S(1)}, bf16[256,2048]{1,0:T(8,128)(2,1)}, u32[]{:S(2)}) copy-start(bf16[256,2048]{1,0:T(8,128)(2,1)} %w_plproj.1) | copy-start | bytes 3145732
  (10 other events, 8.5 us)
Sparse Core Ops, SparseCore 0:
  19.8 30.6 all-gather.2
  62.7 43.3 reduce-scatter.1

commit v2 on v1

--- a/solution.py
+++ b/solution.py
@@ -11,7 +11,7 @@
 
 eps = 1e-06
 rope_base = 1000000.0
-VMEM_BYTES = 40 * 1024 * 1024
+VMEM_BYTES = 60 * 1024 * 1024
 
 
 def rms_scale(values):
@@ -139,20 +139,30 @@
     acc_out[...] = matmul(expo.astype(jnp.bfloat16), values[...])
 
 
-def new_body(place, queries, key, value, acc, top_in, total_in, w_out, part_out):
+def new_body(place, queries, own, first, second, acc, top_in, total_in, w_out, part_out, key, value):
     heads, rows, head_dim = queries.shape
-    new_rows = key.shape[1]
+    new_rows = own.shape[0]
+
+    @pl.when(pl.program_id(0) == 0)
+    def _():
+        for at, source in enumerate((own, first, second)):
+            for which, kept in enumerate((key, value)):
+
+                @pl.when(place[which] == at)
+                def _(source=source, kept=kept):
+                    kept[...] = source[...]
+
     row_at = lax.broadcasted_iota(jnp.int32, (rows, new_rows), 0) + pl.program_id(0) * rows
     causal = lax.broadcasted_iota(jnp.int32, (rows, new_rows), 1) <= row_at
     sides = []
     for h in range(heads):
-        scores = jnp.where(causal, scores_of(queries[h], key[0]), -jnp.inf)
+        scores = jnp.where(causal, scores_of(queries[h], key[...]), -jnp.inf)
         top_old = top_in[h]
         top = jnp.maximum(top_old, jnp.max(scores, axis=1, keepdims=True))
         expo = jnp.exp(scores - top)
         scale = jnp.exp(top_old - top)
         total = total_in[h] * scale + jnp.sum(expo, axis=1, keepdims=True)
-        mix = acc[h] * scale + matmul(expo.astype(jnp.bfloat16), value[0])
+        mix = acc[h] * scale + matmul(expo.astype(jnp.bfloat16), value[...])
         sides.append((mix / total).astype(jnp.bfloat16))
     attn = jnp.concatenate(sides, axis=1)
     part_out[...] = matmul(attn, w_out[...]).astype(jnp.bfloat16)
@@ -247,7 +257,10 @@
         8 << 20,
     )
 
-    gathered = lax.all_gather(fresh[None], "head", axis=0, tiled=True)
+    first = lax.ppermute(fresh, "head", [(0, 1), (1, 2), (2, 0)])
+    second = lax.ppermute(fresh, "head", [(1, 3), (2, 1), (3, 2)])
+    key_from = jnp.where(head_idx == 0, 0, jnp.where(head_idx == 3, 2, 1))
+    value_from = jnp.where(head_idx == 0, 1, jnp.where(head_idx == 3, 0, 2))
 
     full_seq = call(
         sequence_body,
@@ -265,12 +278,12 @@
             pltpu.SemaphoreType.DMA((n_pages,)),
         ],
     )
+    place = jnp.stack([length, kv_of, kv_of + kv_heads])
+    flat = local_heads * new_rows
+    queries, full_seq = lax.optimization_barrier((queries, full_seq))
     spread = lax.all_to_all(
         full_seq.reshape(blocks, block_span, head_dim), "blk", split_axis=0, concat_axis=0, tiled=True
     )
-
-    place = jnp.stack([length, kv_of, kv_of + kv_heads])
-    flat = local_heads * new_rows
     q_tile = flat // 4
     q_rows = lambda cols: pl.BlockSpec((q_tile, cols), lambda i, *_: (i, 0))
     acc, top, total = call(
@@ -285,7 +298,7 @@
         (q_rows(head_dim), q_rows(1), q_rows(1)),
         [table, place],
         [queries.reshape(flat, head_dim), kv_pool],
-        8 * flat * prefix_max * head_dim,
+        10 << 30,
         8 << 20,
         [
             pltpu.VMEM((prefix_max, head_dim), bf16),
@@ -301,27 +314,31 @@
         (new_rows // tile,),
         [
             heads_of(head_dim),
-            pl.BlockSpec((1, new_rows, head_dim), lambda i, p: (p[1], 0, 0)),
-            pl.BlockSpec((1, new_rows, head_dim), lambda i, p: (p[2], 0, 0)),
+            whole((new_rows, head_dim)),
+            whole((new_rows, head_dim)),
+            whole((new_rows, head_dim)),
             heads_of(head_dim),
             heads_of(1),
             heads_of(1),
             whole(w_out.shape),
         ],
         rows_of(width),
-        [place],
+        [jnp.stack([key_from, value_from]).astype(jnp.int32)],
         [
             queries,
-            gathered,
-            gathered,
+            fresh,
+            first,
+            second,
             acc.reshape(local_heads, new_rows, head_dim),
             top.reshape(local_heads, new_rows, 1),
             total.reshape(local_heads, new_rows, 1),
             w_out,
         ],
-        8 * flat * new_rows * head_dim,
+        6 << 30,
         8 << 20,
-    )
+        [pltpu.VMEM((new_rows, head_dim), bf16), pltpu.VMEM((new_rows, head_dim), bf16)],
+    )
+    part, spread = lax.optimization_barrier((part, spread))
     proj_rows = lax.psum_scatter(part, "head", scatter_dimension=0, tiled=True)
 
     quarter = new_rows // lax.axis_size("head")

time: 120 us -> 115 us (0.958)
  Pallas kernels: 24 us -> 67 us
  local copies, waits for them, and re-layouts: 24.5 us -> 3.71 us
  waiting for transfers between devices: 31.7 us -> 11.2 us
  blocking collectives: 18.8 us -> 0 us
  starting transfers between devices: 4.34 us -> 13.5 us
  other arithmetic: 1.15 us -> 3.6 us
    pallas_call x7, Pallas kernels: 24 us -> 67 us  [call(): pl.pallas_call(body, out_shape=out_shape, grid_spec=pltpu.PrefetchScalarG...]
    unnamed x64 -> x10, local copies, waits for them, and re-layouts: 24.5 us -> 3.71 us
    all_gather x1 -> x0, waiting for transfers between devices: 19.1 us -> none  [on_device(): gathered = lax.all_gather(fresh[None], 'head', axis=0, tiled=True)]
    all_to_all x1 -> x0, blocking collectives: 18.8 us -> none  [on_device(): lax.all_to_all(full_seq.reshape(blocks, block_span, head_dim), 'blk', spl...]
    ppermute x0 -> x2, starting transfers between devices: none -> 5.61 us  [the longest x1 4.93 us: on_device(): first = lax.ppermute(fresh, 'head', [(0, 1), (1, 2), (2, 0)])]
    all_to_all x0 -> x1, starting transfers between devices: none -> 3.72 us  [on_device(): lax.all_to_all(full_seq.reshape(blocks, block_span, head_dim), 'blk', spl...]
    all_to_all x1, waiting for transfers between devices: 12.5 us -> 11.2 us  [on_device(): lax.all_to_all(arranged, 'blk', split_axis=0, concat_axis=0, tiled=True)]
  transfers between devices with their start and end apart: 3 -> 5, of which waited for: 3 -> 1; matrix products, arithmetic and copies ran while one was open for 0% -> 2% of each run, Pallas kernels for 11% -> 50%
where the time goes in v2:
time: 115 us; the launch traced here: 114 us
  Pallas kernels  67 us (58%)
  between operations  14.8 us (13%)
  starting transfers between devices  13.5 us (12%)
  waiting for transfers between devices  11.2 us (10%)
  local copies, waits for them, and re-layouts  3.71 us (3%)
  other arithmetic  3.6 us (3%)
    pallas_call x7, Pallas kernels, call(): pl.pallas_call(body, out_shape=out_shape, grid_spec=pltpu.PrefetchScalarG...  67 us
    all_to_all x1, waiting for transfers between devices, on_device(): lax.all_to_all(arranged, 'blk', split_axis=0, concat_axis=0, tiled=True)  11.2 us
    ppermute x1, starting transfers between devices, on_device(): first = lax.ppermute(fresh, 'head', [(0, 1), (1, 2), (2, 0)])  4.93 us
    all_to_all x1, starting transfers between devices, on_device(): lax.all_to_all(arranged, 'blk', split_axis=0, concat_axis=0, tiled=True)  4.15 us
    all_to_all x1, starting transfers between devices, on_device(): lax.all_to_all(full_seq.reshape(blocks, block_span, head_dim), 'blk', spl...  3.72 us
    unnamed x10, local copies, waits for them, and re-layouts  3.71 us
  transfers between devices with their start and end apart: 5, of which 1 were waited for; matrix products, arithmetic and copies ran while one was open for 2% of the time, Pallas kernels for 50%

profile of v2, /device:TPU:0, one launch (start us, length us, event | category | flops | bytes accessed | tf_op | source)
XLA Modules:
  0.0 113.8 jit_solution(9245968111832422268)
XLA Ops:
  7.9 1.8 %multiply_sine_fusion = (f32[512,128]{1,0:T(8,128)}, f32[512,128]{1,0:T(8,128)}) fusion(f32[128]{0:T(128)S(1)} %multiply_power_fusion, f32[512]{0:T(512)S(1)} %add_convert_fusion), kind=kLoop, calls=%fused_computation | loop fusion | flops 65536 | bytes 526848 | tf_op jit(solution)/shard_map/sin | solution.py:229
  9.7 5.8 %shard_map.195 = (bf16[2,512,256]{2,1,0:T(8,128)(2,1)}, bf16[512,256]{1,0:T(8,128)(2,1)}) custom-call(s32[1]{0:T(128)} %bitcast.5.is_key, bf16[512,2048]{1,0:T(8,128)(2,1)} %hidden.3, f32[1,2048]{1,0:T(1,128)} %bitcast.23, bf16[2048,512]{1,0:T(8,128)(2,1)} %w_query.1, bf16[2048,256]{1,0:T(8,128)(2,1)} %w_keyval.1, f32[1,256]{1,0:T(1,128)} %bitcast.30, ...), custom_call_target="tpu_custom_call" | custom-call | flops 1610612736 | bytes 8388608 | tf_op jit(solution)/shard_map/pallas_call | solution.py:37
  15.5 4.9 %collective-permute-start = (bf16[512,256]{1,0:T(8,128)(2,1)}, bf16[512,256]{1,0:T(8,128)(2,1)S(1)}, u32[]{:S(2)}, u32[]{:S(2)}) collective-permute-start(bf16[512,256]{1,0:T(8,128)(2,1)} %get-tuple-element.12.fresh.own), channel_id=1, source_target_pairs={{0,1},{1,2},{2,0},{4,5},{5,6},{6,4},{8,9},{9,10},{10,8},{12,13},{1... | collective-permute-start | bytes 786440 | tf_op jit(solution)/shard_map/ppermute | solution.py:260
  20.4 0.7 collective-permute-start.1
  21.1 0.6 pad_add_fusion.1.place
  21.7 4.1 %shard_map.196 = bf16[2048,256]{1,0:T(8,128)(2,1)} custom-call(s32[12]{0:T(128)} %bitcast.28, s32[2]{0:T(128)} %pad_add_fusion.1.place, bf16[512,256]{1,0:T(8,128)(2,1)} %get-tuple-element.12.fresh.own, bf16[12,4,128,256]{3,2,1,0:T(8,128)(2,1)} %pool.3), custom_call_target="tpu_custom_call" | custom-call | flops 1048576 | bytes 4194304 | tf_op jit(solution)/shard_map/pallas_call | solution.py:37
  25.8 3.7 %all-to-all-start = ((bf16[8,256,256]{2,1,0:T(8,128)(2,1)}), bf16[8,256,256]{2,1,0:T(8,128)(2,1)S(1)}, u32[]{:S(2)}, u32[]{:S(2)}) async-start(bf16[8,256,256]{2,1,0:T(8,128)(2,1)} %bitcast.21), calls=%async_computation | async-start | bytes 2097152 | tf_op jit(solution)/shard_map/all_to_all | solution.py:284
  29.5 0.0 reduce-scatter.2.cloned.1.call-start
  29.6 0.6 pad_add_fusion.2.place
  30.1 9.0 %shard_map.197 = (f32[1024,256]{1,0:T(8,128)}, f32[1024,1]{1,0:T(8,128)}, f32[1024,1]{1,0:T(8,128)}) custom-call(s32[12]{0:T(128)} %bitcast.29, s32[3]{0:T(128)} %pad_add_fusion.2.place, bf16[1024,256]{1,0:T(8,128)(2,1)} %bitcast.33, bf16[12,4,128,256]{3,2,1,0:T(8,128)(2,1)} %pool.3), custom_call_target="tpu_custom_call" | custom-call | flops 10737418240 | bytes 8388608 | tf_op jit(solution)/shard_map/pallas_call | solution.py:37
  39.2 0.6 pad_add_fusion.place
  39.8 0.7 copy-done.2
  40.5 0.1 copy-done.3
  40.6 7.1 %shard_map.198 = bf16[512,2048]{1,0:T(8,128)(2,1)} custom-call(s32[2]{0:T(128)} %pad_add_fusion.place, bf16[2,512,256]{2,1,0:T(8,128)(2,1)} %get-tuple-element.13.queries, bf16[512,256]{1,0:T(8,128)(2,1)} %get-tuple-element.12.fresh.own, bf16[512,256]{1,0:T(8,128)(2,1)} %copy-done.2, bf16[512,256]{1,0:T(8,128)(2,1)} %copy-done.3, f32[2,512,256]{2,1,0:T(8,128)} %bitcast.32, ...), custom_call_target="tpu_custom_call" | custom-call | flops 6442450944 | bytes 8388608 | tf_op jit(solution)/shard_map/pallas_call | solution.py:37
  47.7 0.0 copy-start
  47.7 0.0 reduce-scatter.2.cloned.1.call-update
  47.7 0.9 copy-done
  48.7 33.7 %shard_map.200 = bf16[8,256,256]{2,1,0:T(8,128)(2,1)} custom-call(s32[8]{0:T(128)} %owner.1, bf16[8,256,256]{2,1,0:T(8,128)(2,1)} %copy-done), custom_call_target="tpu_custom_call" | custom-call | flops 1024 | bytes 2097152 | tf_op jit(solution)/shard_map/pallas_call | solution.py:37
  82.4 4.2 %all-to-all-start.1 = ((bf16[8,256,256]{2,1,0:T(8,128)(2,1)}), bf16[8,256,256]{2,1,0:T(8,128)(2,1)S(1)}, u32[]{:S(2)}, u32[]{:S(2)}) async-start(bf16[8,256,256]{2,1,0:T(8,128)(2,1)} %shard_map.200), calls=%async_computation.2 | async-start | bytes 2097152 | tf_op jit(solution)/shard_map/all_to_all | solution.py:377
  86.6 1.0 copy.21.left
  87.6 3.2 %shard_map.194.base = f32[128,2048]{1,0:T(8,128)} custom-call(s32[1]{0:T(128)} %bitcast.place, bf16[512,2048]{1,0:T(8,128)(2,1)} %hidden.3, f32[1,2048]{1,0:T(1,128)} %bitcast.24, bf16[2048,64]{1,0:T(8,128)(2,1)} %copy.21.left, bf16[64,2048]{1,0:T(8,128)(2,1)} %right.1, f32[1,2048]{1,0:T(1,128)} %bitcast.25), custom_call_target="tpu_custom_call" | custom-call | flops 268435456 | bytes 4194304 | tf_op jit(solution)/shard_map/pallas_call | solution.py:37
  90.8 11.2 %all-to-all-done.1 = bf16[8,256,256]{2,1,0:T(8,128)(2,1)S(1)} async-done(((bf16[8,256,256]{2,1,0:T(8,128)(2,1)}), bf16[8,256,256]{2,1,0:T(8,128)(2,1)S(1)}, u32[]{:S(2)}, u32[]{:S(2)}) %all-to-all-start.1) | async-done | bytes 1048608 | tf_op jit(solution)/shard_map/all_to_all | solution.py:377
  102.0 4.0 %shard_map.199 = bf16[128,2048]{1,0:T(8,128)(2,1)} custom-call(f32[128,2048]{1,0:T(8,128)} %shard_map.194.base, bf16[128,2048]{1,0:T(8,128)(2,1)} %reduce-scatter.2.cloned.1.call-done.proj, f32[1,2048]{1,0:T(1,128)} %bitcast.26, bf16[128,256]{1,0:T(8,128)(2,1)} %layer_input.1, bf16[2048,256]{1,0:T(8,128)(2,1)} %w_plgate.1, bf16[256,2048]{1,0:T(8,128)(2,1)} %w_plproj.1, ...), custom_call_target="tpu_custom_call" | custom-call | flops 268435456 | bytes 6291456 | tf_op jit(solution)/shard_map/pallas_call | solution.py:37
  106.0 1.0 copy.24
  (10 shorter events, 0.0 us)
Async XLA Ops:
  15.5 24.3 %collective-permute-start = (bf16[512,256]{1,0:T(8,128)(2,1)}, bf16[512,256]{1,0:T(8,128)(2,1)S(1)}, u32[]{:S(2)}, u32[]{:S(2)}) collective-permute-start(bf16[512,256]{1,0:T(8,128)(2,1)} %get-tuple-element.12.fresh.own), channel_id=1, source_target_pairs={{0,1},{1,2},{2,0},{4,5},{5,6},{6,4},{8,9},{9,10},{10,8},{12,13},{1... | collective-permute-start | bytes 786440 | tf_op jit(solution)/shard_map/ppermute | solution.py:260
  20.4 19.4 %collective-permute-start.1 = (bf16[512,256]{1,0:T(8,128)(2,1)}, bf16[512,256]{1,0:T(8,128)(2,1)S(1)}, u32[]{:S(2)}, u32[]{:S(2)}) collective-permute-start(bf16[512,256]{1,0:T(8,128)(2,1)} %get-tuple-element.12.fresh.own), channel_id=1, source_target_pairs={{1,3},{2,1},{3,2},{5,7},{6,5},{7,6},{9,11},{10,9},{11,10},{13,15},... | collective-permute-start | bytes 786440 | tf_op jit(solution)/shard_map/ppermute | solution.py:261
  25.8 21.9 %all-to-all-start = ((bf16[8,256,256]{2,1,0:T(8,128)(2,1)}), bf16[8,256,256]{2,1,0:T(8,128)(2,1)S(1)}, u32[]{:S(2)}, u32[]{:S(2)}) async-start(bf16[8,256,256]{2,1,0:T(8,128)(2,1)} %bitcast.21), calls=%async_computation | async-start | bytes 2097152 | tf_op jit(solution)/shard_map/all_to_all | solution.py:284
  29.5 72.5 %reduce-scatter.2.cloned.1.call-start = ((), (), s32[]{:S(2)}) async-start(), calls=%async_computation.3 | async-start | bytes 2621440 | tf_op jit(solution)/shard_map/reduce_scatter | solution.py:342
  39.8 0.7 copy-start.2
  39.8 0.8 copy-start.3
  47.7 1.0 copy-start
  48.7 37.9 %copy-start.1 = (bf16[2048,64]{0,1:T(8,128)(2,1)S(1)}, bf16[2048,64]{0,1:T(8,128)(2,1)}, u32[]{:S(2)}) copy-start(bf16[2048,64]{0,1:T(8,128)(2,1)} %param.28) | copy-start | bytes 786436
  82.4 19.6 %all-to-all-start.1 = ((bf16[8,256,256]{2,1,0:T(8,128)(2,1)}), bf16[8,256,256]{2,1,0:T(8,128)(2,1)S(1)}, u32[]{:S(2)}, u32[]{:S(2)}) async-start(bf16[8,256,256]{2,1,0:T(8,128)(2,1)} %shard_map.200), calls=%async_computation.2 | async-start | bytes 2097152 | tf_op jit(solution)/shard_map/all_to_all | solution.py:377
Sparse Core Ops, SparseCore 0:
  47.8 46.1 reduce-scatter.1

commit v3 on v2

--- a/solution.py
+++ b/solution.py
@@ -93,19 +93,12 @@
     out[prefix:, :] = wide[prefix : prefix + rows, :].astype(jnp.bfloat16)
 
 
-def arrange_body(owner, spread, out, sems):
-    n = spread.shape[0]
-
-    def start(r, carry):
-        pltpu.make_async_copy(spread.at[r], out.at[owner[r]], sems.at[r]).start()
+def arrange_body(owner, spread, out):
+    def move(r, carry):
+        out[owner[r]] = spread[r]
         return carry
 
-    def wait(r, carry):
-        pltpu.make_async_copy(spread.at[r], out.at[owner[r]], sems.at[r]).wait()
-        return carry
-
-    lax.fori_loop(0, n, start, 0)
-    lax.fori_loop(0, n, wait, 0)
+    lax.fori_loop(0, spread.shape[0], move, 0)
 
 
 def old_body(table, place, queries, pool, acc_out, top_out, total_out, keys, values, sems):
@@ -366,13 +359,12 @@
         arrange_body,
         jax.ShapeDtypeStruct(spread.shape, bf16),
         (1,),
-        [in_hbm],
-        in_hbm,
+        [whole(spread.shape)],
+        whole(spread.shape),
         [decode_owner],
         [spread],
         1 << 10,
         2 << 20,
-        [pltpu.SemaphoreType.DMA((blocks,))],
     )
     owned = lax.all_to_all(arranged, "blk", split_axis=0, concat_axis=0, tiled=True)
 

time: 115 us -> 106 us (0.922)
  Pallas kernels: 67 us -> 36.3 us
  waiting for transfers between devices: 11.2 us -> 34 us
    pallas_call x7, Pallas kernels: 67 us -> 36.3 us  [call(): pl.pallas_call(body, out_shape=out_shape, grid_spec=pltpu.PrefetchScalarG...]
    reduce_scatter x1, waiting for transfers between devices: 0.01 us -> 22.8 us  [on_device(): proj_rows = lax.psum_scatter(part, 'head', scatter_dimension=0, tiled=True)]
  transfers between devices with their start and end apart: 5 -> 5, of which waited for: 1 -> 2; matrix products, arithmetic and copies ran while one was open for 2% -> 3% of each run, Pallas kernels for 50% -> 25%
where the time goes in v3:
time: 106 us
  Pallas kernels  36.3 us (34%)
  waiting for transfers between devices  34 us (32%)
  between operations  14.8 us (14%)
  starting transfers between devices  13.5 us (13%)
  local copies, waits for them, and re-layouts  3.71 us (4%)
  other arithmetic  3.6 us (3%)
    pallas_call x7, Pallas kernels, call(): pl.pallas_call(body, out_shape=out_shape, grid_spec=pltpu.PrefetchScalarG...  36.3 us
    reduce_scatter x1, waiting for transfers between devices, on_device(): proj_rows = lax.psum_scatter(part, 'head', scatter_dimension=0, tiled=True)  22.8 us
    all_to_all x1, waiting for transfers between devices, on_device(): lax.all_to_all(arranged, 'blk', split_axis=0, concat_axis=0, tiled=True)  11.2 us
    ppermute x1, starting transfers between devices, on_device(): first = lax.ppermute(fresh, 'head', [(0, 1), (1, 2), (2, 0)])  4.93 us
    all_to_all x1, starting transfers between devices, on_device(): lax.all_to_all(arranged, 'blk', split_axis=0, concat_axis=0, tiled=True)  4.14 us
    all_to_all x1, starting transfers between devices, on_device(): lax.all_to_all(full_seq.reshape(blocks, block_span, head_dim), 'blk', spl...  3.72 us
    unnamed x10, local copies, waits for them, and re-layouts  3.71 us
  transfers between devices with their start and end apart: 5, of which 2 were waited for; matrix products, arithmetic and copies ran while one was open for 3% of the time, Pallas kernels for 25%

profile of v3, /device:TPU:0, one launch (start us, length us, event | category | flops | bytes accessed | tf_op | source)
XLA Modules:
  0.0 105.9 jit_solution(6955082223404499129)
XLA Ops:
  7.9 1.8 %multiply_sine_fusion = (f32[512,128]{1,0:T(8,128)}, f32[512,128]{1,0:T(8,128)}) fusion(f32[128]{0:T(128)S(1)} %multiply_power_fusion, f32[512]{0:T(512)S(1)} %add_convert_fusion), kind=kLoop, calls=%fused_computation | loop fusion | flops 65536 | bytes 526848 | tf_op jit(solution)/shard_map/sin | solution.py:222
  9.7 5.8 %shard_map.195 = (bf16[2,512,256]{2,1,0:T(8,128)(2,1)}, bf16[512,256]{1,0:T(8,128)(2,1)}) custom-call(s32[1]{0:T(128)} %bitcast.5.is_key, bf16[512,2048]{1,0:T(8,128)(2,1)} %hidden.3, f32[1,2048]{1,0:T(1,128)} %bitcast.23, bf16[2048,512]{1,0:T(8,128)(2,1)} %w_query.1, bf16[2048,256]{1,0:T(8,128)(2,1)} %w_keyval.1, f32[1,256]{1,0:T(1,128)} %bitcast.30, ...), custom_call_target="tpu_custom_call" | custom-call | flops 1610612736 | bytes 8388608 | tf_op jit(solution)/shard_map/pallas_call | solution.py:37
  15.5 4.9 %collective-permute-start = (bf16[512,256]{1,0:T(8,128)(2,1)}, bf16[512,256]{1,0:T(8,128)(2,1)S(1)}, u32[]{:S(2)}, u32[]{:S(2)}) collective-permute-start(bf16[512,256]{1,0:T(8,128)(2,1)} %get-tuple-element.12.fresh.own), channel_id=1, source_target_pairs={{0,1},{1,2},{2,0},{4,5},{5,6},{6,4},{8,9},{9,10},{10,8},{12,13},{1... | collective-permute-start | bytes 786440 | tf_op jit(solution)/shard_map/ppermute | solution.py:253
  20.4 0.7 collective-permute-start.1
  21.1 0.6 pad_add_fusion.1.place
  21.7 4.1 %shard_map.196 = bf16[2048,256]{1,0:T(8,128)(2,1)} custom-call(s32[12]{0:T(128)} %bitcast.28, s32[2]{0:T(128)} %pad_add_fusion.1.place, bf16[512,256]{1,0:T(8,128)(2,1)} %get-tuple-element.12.fresh.own, bf16[12,4,128,256]{3,2,1,0:T(8,128)(2,1)} %pool.3), custom_call_target="tpu_custom_call" | custom-call | flops 1048576 | bytes 4194304 | tf_op jit(solution)/shard_map/pallas_call | solution.py:37
  25.8 3.7 %all-to-all-start = ((bf16[8,256,256]{2,1,0:T(8,128)(2,1)}), bf16[8,256,256]{2,1,0:T(8,128)(2,1)S(1)}, u32[]{:S(2)}, u32[]{:S(2)}) async-start(bf16[8,256,256]{2,1,0:T(8,128)(2,1)} %bitcast.21), calls=%async_computation | async-start | bytes 2097152 | tf_op jit(solution)/shard_map/all_to_all | solution.py:277
  29.5 0.0 reduce-scatter.2.cloned.1.call-start
  29.6 0.6 pad_add_fusion.2.place
  30.1 9.0 %shard_map.197 = (f32[1024,256]{1,0:T(8,128)}, f32[1024,1]{1,0:T(8,128)}, f32[1024,1]{1,0:T(8,128)}) custom-call(s32[12]{0:T(128)} %bitcast.29, s32[3]{0:T(128)} %pad_add_fusion.2.place, bf16[1024,256]{1,0:T(8,128)(2,1)} %bitcast.33, bf16[12,4,128,256]{3,2,1,0:T(8,128)(2,1)} %pool.3), custom_call_target="tpu_custom_call" | custom-call | flops 10737418240 | bytes 8388608 | tf_op jit(solution)/shard_map/pallas_call | solution.py:37
  39.2 0.6 pad_add_fusion.place
  39.8 0.7 copy-done.2
  40.5 0.1 copy-done.3
  40.6 7.1 %shard_map.198 = bf16[512,2048]{1,0:T(8,128)(2,1)} custom-call(s32[2]{0:T(128)} %pad_add_fusion.place, bf16[2,512,256]{2,1,0:T(8,128)(2,1)} %get-tuple-element.13.queries, bf16[512,256]{1,0:T(8,128)(2,1)} %get-tuple-element.12.fresh.own, bf16[512,256]{1,0:T(8,128)(2,1)} %copy-done.2, bf16[512,256]{1,0:T(8,128)(2,1)} %copy-done.3, f32[2,512,256]{2,1,0:T(8,128)} %bitcast.32, ...), custom_call_target="tpu_custom_call" | custom-call | flops 6442450944 | bytes 8388608 | tf_op jit(solution)/shard_map/pallas_call | solution.py:37
  47.7 0.0 reduce-scatter.2.cloned.1.call-update
  47.7 0.9 copy-done
  48.7 3.1 %shard_map.200 = bf16[8,256,256]{2,1,0:T(8,128)(2,1)} custom-call(s32[8]{0:T(128)} %owner.1, bf16[8,256,256]{2,1,0:T(8,128)(2,1)} %copy-done), custom_call_target="tpu_custom_call" | custom-call | flops 1024 | bytes 2097152 | tf_op jit(solution)/shard_map/pallas_call | solution.py:37
  51.7 4.1 %all-to-all-start.1 = ((bf16[8,256,256]{2,1,0:T(8,128)(2,1)}), bf16[8,256,256]{2,1,0:T(8,128)(2,1)S(1)}, u32[]{:S(2)}, u32[]{:S(2)}) async-start(bf16[8,256,256]{2,1,0:T(8,128)(2,1)} %shard_map.200), calls=%async_computation.2 | async-start | bytes 2097152 | tf_op jit(solution)/shard_map/all_to_all | solution.py:369
  55.9 1.0 copy.21.left
  56.9 3.2 %shard_map.194.base = f32[128,2048]{1,0:T(8,128)} custom-call(s32[1]{0:T(128)} %bitcast.place, bf16[512,2048]{1,0:T(8,128)(2,1)} %hidden.3, f32[1,2048]{1,0:T(1,128)} %bitcast.24, bf16[2048,64]{1,0:T(8,128)(2,1)} %copy.21.left, bf16[64,2048]{1,0:T(8,128)(2,1)} %right.1, f32[1,2048]{1,0:T(1,128)} %bitcast.25), custom_call_target="tpu_custom_call" | custom-call | flops 268435456 | bytes 4194304 | tf_op jit(solution)/shard_map/pallas_call | solution.py:37
  60.1 11.2 %all-to-all-done.1 = bf16[8,256,256]{2,1,0:T(8,128)(2,1)S(1)} async-done(((bf16[8,256,256]{2,1,0:T(8,128)(2,1)}), bf16[8,256,256]{2,1,0:T(8,128)(2,1)S(1)}, u32[]{:S(2)}, u32[]{:S(2)}) %all-to-all-start.1) | async-done | bytes 1048608 | tf_op jit(solution)/shard_map/all_to_all | solution.py:369
  71.3 22.8 %reduce-scatter.2.cloned.1.call-done.proj = bf16[128,2048]{1,0:T(8,128)(2,1)} async-done(((bf16[512,2048]{1,0:T(8,128)(2,1)}), bf16[128,2048]{1,0:T(8,128)(2,1)}) %reduce-scatter.2.cloned.1.call-update) | async-done | bytes 524304 | tf_op jit(solution)/shard_map/reduce_scatter | solution.py:335
  94.1 4.0 %shard_map.199 = bf16[128,2048]{1,0:T(8,128)(2,1)} custom-call(f32[128,2048]{1,0:T(8,128)} %shard_map.194.base, bf16[128,2048]{1,0:T(8,128)(2,1)} %reduce-scatter.2.cloned.1.call-done.proj, f32[1,2048]{1,0:T(1,128)} %bitcast.26, bf16[128,256]{1,0:T(8,128)(2,1)} %layer_input.1, bf16[2048,256]{1,0:T(8,128)(2,1)} %w_plgate.1, bf16[256,2048]{1,0:T(8,128)(2,1)} %w_plproj.1, ...), custom_call_target="tpu_custom_call" | custom-call | flops 268435456 | bytes 6291456 | tf_op jit(solution)/shard_map/pallas_call | solution.py:37
  98.1 1.0 copy.24
  (10 shorter events, 0.0 us)
Async XLA Ops:
  15.5 24.3 %collective-permute-start = (bf16[512,256]{1,0:T(8,128)(2,1)}, bf16[512,256]{1,0:T(8,128)(2,1)S(1)}, u32[]{:S(2)}, u32[]{:S(2)}) collective-permute-start(bf16[512,256]{1,0:T(8,128)(2,1)} %get-tuple-element.12.fresh.own), channel_id=1, source_target_pairs={{0,1},{1,2},{2,0},{4,5},{5,6},{6,4},{8,9},{9,10},{10,8},{12,13},{1... | collective-permute-start | bytes 786440 | tf_op jit(solution)/shard_map/ppermute | solution.py:253
  20.4 19.4 %collective-permute-start.1 = (bf16[512,256]{1,0:T(8,128)(2,1)}, bf16[512,256]{1,0:T(8,128)(2,1)S(1)}, u32[]{:S(2)}, u32[]{:S(2)}) collective-permute-start(bf16[512,256]{1,0:T(8,128)(2,1)} %get-tuple-element.12.fresh.own), channel_id=1, source_target_pairs={{1,3},{2,1},{3,2},{5,7},{6,5},{7,6},{9,11},{10,9},{11,10},{13,15},... | collective-permute-start | bytes 786440 | tf_op jit(solution)/shard_map/ppermute | solution.py:254
  25.8 21.9 %all-to-all-start = ((bf16[8,256,256]{2,1,0:T(8,128)(2,1)}), bf16[8,256,256]{2,1,0:T(8,128)(2,1)S(1)}, u32[]{:S(2)}, u32[]{:S(2)}) async-start(bf16[8,256,256]{2,1,0:T(8,128)(2,1)} %bitcast.21), calls=%async_computation | async-start | bytes 2097152 | tf_op jit(solution)/shard_map/all_to_all | solution.py:277
  29.5 64.6 %reduce-scatter.2.cloned.1.call-start = ((), (), s32[]{:S(2)}) async-start(), calls=%async_computation.3 | async-start | bytes 2621440 | tf_op jit(solution)/shard_map/reduce_scatter | solution.py:335
  39.8 0.7 copy-start.2
  39.8 0.8 copy-start.3
  47.7 1.0 copy-start
  48.7 7.2 %copy-start.1 = (bf16[2048,64]{0,1:T(8,128)(2,1)S(1)}, bf16[2048,64]{0,1:T(8,128)(2,1)}, u32[]{:S(2)}) copy-start(bf16[2048,64]{0,1:T(8,128)(2,1)} %param.28) | copy-start | bytes 786436
  51.7 19.6 %all-to-all-start.1 = ((bf16[8,256,256]{2,1,0:T(8,128)(2,1)}), bf16[8,256,256]{2,1,0:T(8,128)(2,1)S(1)}, u32[]{:S(2)}, u32[]{:S(2)}) async-start(bf16[8,256,256]{2,1,0:T(8,128)(2,1)} %shard_map.200), calls=%async_computation.2 | async-start | bytes 2097152 | tf_op jit(solution)/shard_map/all_to_all | solution.py:369
Sparse Core Ops, SparseCore 0:
  47.8 46.1 reduce-scatter.1

commit v4 on v3

--- a/solution.py
+++ b/solution.py
@@ -174,6 +174,22 @@
     gate = jax.nn.gelu(matmul(state.astype(jnp.bfloat16), w_plgate[...]), approximate=True)
     gated = (gate * layer_input[...].astype(jnp.float32)).astype(jnp.bfloat16)
     out[...] = (state + rms_scale(matmul(gated, w_plproj[...])) * pl_gain[...]).astype(jnp.bfloat16)
+
+
+def line_scatter(part, here, n, rows):
+    def share(at):
+        start = jnp.clip(at, 0, n - 1) * rows
+        return lax.dynamic_slice_in_dim(part, start, rows, 0).astype(jnp.float32)
+
+    up = jnp.zeros((), jnp.float32)
+    down = jnp.zeros((), jnp.float32)
+    for k in range(n - 1):
+        send_up = (share(n - 1 - k + here) + up).astype(jnp.bfloat16)
+        send_down = (share(k + here - n + 1) + down).astype(jnp.bfloat16)
+        up = lax.ppermute(send_up, "head", [(z, z + 1) for z in range(k + 1)])
+        down = lax.ppermute(send_down, "head", [(n - 1 - z, n - 2 - z) for z in range(k + 1)])
+        up, down = up.astype(jnp.float32), down.astype(jnp.float32)
+    return (share(here) + up + down).astype(jnp.bfloat16)
 
 
 def on_device(
@@ -332,9 +348,9 @@
         [pltpu.VMEM((new_rows, head_dim), bf16), pltpu.VMEM((new_rows, head_dim), bf16)],
     )
     part, spread = lax.optimization_barrier((part, spread))
-    proj_rows = lax.psum_scatter(part, "head", scatter_dimension=0, tiled=True)
-
     quarter = new_rows // lax.axis_size("head")
+    proj_rows = line_scatter(part, head_idx, lax.axis_size("head"), quarter)
+
     rank = laurel_left.shape[1]
     gate_dim = w_plgate.shape[1]
     base = call(

time: 106 us -> 121 us (1.14)
  starting transfers between devices: 13.5 us -> 33 us
  between operations: 14.8 us -> 1.42 us
  other arithmetic: 3.6 us -> 12.5 us
  waiting for transfers between devices: 34 us -> 31.3 us
  local copies, waits for them, and re-layouts: 3.71 us -> 5.48 us
    ppermute x0 -> x6, waiting for transfers between devices: none -> 28.5 us  [the longest x3 21.4 us: line_scatter(): up = lax.ppermute(send_up, 'head', [(z, z + 1) for z in range(k + 1)])]
    reduce_scatter x1 -> x0, waiting for transfers between devices: 22.8 us -> none  [on_device(): proj_rows = lax.psum_scatter(part, 'head', scatter_dimension=0, tiled=True)]
    ppermute x0 -> x6, starting transfers between devices: none -> 20 us  [the longest x3 15.8 us: line_scatter(): up = lax.ppermute(send_up, 'head', [(z, z + 1) for z in range(k + 1)])]
    convert_element_type x0 -> x4, other arithmetic: none -> 8.73 us  [the longest x2 4.52 us: line_scatter(): send_up = (share(n - 1 - k + here) + up).astype(jnp.bfloat16)]
    all_to_all x1, waiting for transfers between devices: 11.2 us -> 2.77 us  [on_device(): lax.all_to_all(arranged, 'blk', split_axis=0, concat_axis=0, tiled=True)]
    dynamic_slice x0 -> x1, local copies, waits for them, and re-layouts: none -> 2.7 us  [share(): return lax.dynamic_slice_in_dim(part, start, rows, 0).astype(jnp.float32)]
    unnamed x10 -> x12, local copies, waits for them, and re-layouts: 3.71 us -> 2.78 us
  transfers between devices with their start and end apart: 5 -> 10, of which waited for: 2 -> 5; matrix products, arithmetic and copies ran while one was open for 3% -> 6% of each run, Pallas kernels for 25% -> 22%
where the time goes in v4:
time: 121 us; the launch traced here: 120 us
  Pallas kernels  36.2 us (30%)
  starting transfers between devices  33 us (27%)
  waiting for transfers between devices  31.3 us (26%)
  other arithmetic  12.5 us (10%)
  local copies, waits for them, and re-layouts  5.48 us (5%)
  between operations  1.42 us (1%)
    pallas_call x7, Pallas kernels, call(): pl.pallas_call(body, out_shape=out_shape, grid_spec=pltpu.PrefetchScalarG...  36.2 us
    ppermute x3, waiting for transfers between devices, line_scatter(): up = lax.ppermute(send_up, 'head', [(z, z + 1) for z in range(k + 1)])  21.4 us
    ppermute x3, starting transfers between devices, line_scatter(): up = lax.ppermute(send_up, 'head', [(z, z + 1) for z in range(k + 1)])  15.8 us
    ppermute x3, waiting for transfers between devices, line_scatter(): lax.ppermute(send_down, 'head', [(n - 1 - z, n - 2 - z) for z in range(k...  7.1 us
    ppermute x1, starting transfers between devices, on_device(): first = lax.ppermute(fresh, 'head', [(0, 1), (1, 2), (2, 0)])  4.92 us
    convert_element_type x2, other arithmetic, line_scatter(): send_up = (share(n - 1 - k + here) + up).astype(jnp.bfloat16)  4.52 us
    ppermute x3, starting transfers between devices, line_scatter(): lax.ppermute(send_down, 'head', [(n - 1 - z, n - 2 - z) for z in range(k...  4.18 us
    all_to_all x1, starting transfers between devices, on_device(): lax.all_to_all(full_seq.reshape(blocks, block_span, head_dim), 'blk', spl...  3.74 us
  transfers between devices with their start and end apart: 10, of which 5 were waited for; matrix products, arithmetic and copies ran while one was open for 6% of the time, Pallas kernels for 22%

profile of v4, /device:TPU:0, one launch (start us, length us, event | category | flops | bytes accessed | tf_op | source)
XLA Modules:
  0.0 119.8 jit_solution(17453689730230885020)
XLA Ops:
  1.3 1.8 %multiply_sine_fusion = (f32[512,128]{1,0:T(8,128)}, f32[512,128]{1,0:T(8,128)}) fusion(f32[128]{0:T(128)S(1)} %multiply_power_fusion, f32[512]{0:T(512)S(1)} %add_convert_fusion.5), kind=kLoop, calls=%fused_computation.5 | loop fusion | flops 65536 | bytes 526848 | tf_op jit(solution)/shard_map/sin | solution.py:238
  3.1 5.9 %shard_map.195 = (bf16[2,512,256]{2,1,0:T(8,128)(2,1)}, bf16[512,256]{1,0:T(8,128)(2,1)}) custom-call(s32[1]{0:T(128)} %bitcast.5.is_key, bf16[512,2048]{1,0:T(8,128)(2,1)} %hidden.3, f32[1,2048]{1,0:T(1,128)} %bitcast.23, bf16[2048,512]{1,0:T(8,128)(2,1)} %w_query.1, bf16[2048,256]{1,0:T(8,128)(2,1)} %w_keyval.1, f32[1,256]{1,0:T(1,128)} %bitcast.30, ...), custom_call_target="tpu_custom_call" | custom-call | flops 1610612736 | bytes 8388608 | tf_op jit(solution)/shard_map/pallas_call | solution.py:37
  9.0 4.9 %collective-permute-start = (bf16[512,256]{1,0:T(8,128)(2,1)}, bf16[512,256]{1,0:T(8,128)(2,1)S(1)}, u32[]{:S(2)}, u32[]{:S(2)}) collective-permute-start(bf16[512,256]{1,0:T(8,128)(2,1)} %get-tuple-element.12.fresh.own), channel_id=1, source_target_pairs={{0,1},{1,2},{2,0},{4,5},{5,6},{6,4},{8,9},{9,10},{10,8},{12,13},{1... | collective-permute-start | bytes 786440 | tf_op jit(solution)/shard_map/ppermute | solution.py:269
  15.2 4.1 %shard_map.196 = bf16[2048,256]{1,0:T(8,128)(2,1)} custom-call(s32[12]{0:T(128)} %bitcast.28, s32[2]{0:T(128)} %pad_add_fusion.1.place, bf16[512,256]{1,0:T(8,128)(2,1)} %get-tuple-element.12.fresh.own, bf16[12,4,128,256]{3,2,1,0:T(8,128)(2,1)} %pool.3), custom_call_target="tpu_custom_call" | custom-call | flops 1048576 | bytes 4194304 | tf_op jit(solution)/shard_map/pallas_call | solution.py:37
  19.3 3.7 %all-to-all-start = ((bf16[8,256,256]{2,1,0:T(8,128)(2,1)}), bf16[8,256,256]{2,1,0:T(8,128)(2,1)S(1)}, u32[]{:S(2)}, u32[]{:S(2)}) async-start(bf16[8,256,256]{2,1,0:T(8,128)(2,1)} %bitcast.21), calls=%async_computation | async-start | bytes 2097152 | tf_op jit(solution)/shard_map/all_to_all | solution.py:293
  23.6 9.0 %shard_map.197 = (f32[1024,256]{1,0:T(8,128)}, f32[1024,1]{1,0:T(8,128)}, f32[1024,1]{1,0:T(8,128)}) custom-call(s32[12]{0:T(128)} %bitcast.29, s32[3]{0:T(128)} %pad_add_fusion.2.place, bf16[1024,256]{1,0:T(8,128)(2,1)} %bitcast.33, bf16[12,4,128,256]{3,2,1,0:T(8,128)(2,1)} %pool.3), custom_call_target="tpu_custom_call" | custom-call | flops 10737418240 | bytes 8388608 | tf_op jit(solution)/shard_map/pallas_call | solution.py:37
  34.2 7.0 %shard_map.198 = bf16[512,2048]{1,0:T(8,128)(2,1)} custom-call(s32[2]{0:T(128)} %pad_add_fusion.place, bf16[2,512,256]{2,1,0:T(8,128)(2,1)} %get-tuple-element.13.queries, bf16[512,256]{1,0:T(8,128)(2,1)} %get-tuple-element.12.fresh.own, bf16[512,256]{1,0:T(8,128)(2,1)} %copy-done.3, bf16[512,256]{1,0:T(8,128)(2,1)} %copy-done.4, f32[2,512,256]{2,1,0:T(8,128)} %bitcast.32, ...), custom_call_target="tpu_custom_call" | custom-call | flops 6442450944 | bytes 8388608 | tf_op jit(solution)/shard_map/pallas_call | solution.py:37
  41.2 2.7 %constant_dynamic-slice_fusion.1 = (bf16[128,2048]{1,0:T(8,128)(2,1)}, bf16[128,2048]{1,0:T(8,128)(2,1)}) fusion(bf16[512,2048]{1,0:T(8,128)(2,1)} %shard_map.198, s32[]{:T(128)S(6)} %select_n.48, s32[]{:T(128)S(6)} %select_n.51), kind=kLoop, calls=%fused_computation.9 | loop fusion | bytes 2097160 | tf_op jit(solution)/shard_map/dynamic_slice | solution.py:182
  43.9 5.5 %collective-permute-start.2 = (bf16[128,2048]{1,0:T(8,128)(2,1)}, bf16[128,2048]{1,0:T(8,128)(2,1)}, u32[]{:S(2)}, u32[]{:S(2)}) collective-permute-start(bf16[128,2048]{1,0:T(8,128)(2,1)} %get-tuple-element.22), channel_id=1, source_target_pairs={{0,1},{4,5},{8,9},{12,13},{16,17},{20,21},{24,25},{28,29}} | collective-permute-start | bytes 1572872 | tf_op jit(solution)/shard_map/ppermute | solution.py:189
  49.4 1.5 %collective-permute-start.5 = (bf16[128,2048]{1,0:T(8,128)(2,1)}, bf16[128,2048]{1,0:T(8,128)(2,1)}, u32[]{:S(2)}, u32[]{:S(2)}) collective-permute-start(bf16[128,2048]{1,0:T(8,128)(2,1)} %get-tuple-element.23), channel_id=1, source_target_pairs={{3,2},{7,6},{11,10},{15,14},{19,18},{23,22},{27,26},{31,30}} | collective-permute-start | bytes 1572872 | tf_op jit(solution)/shard_map/ppermute | solution.py:190
  50.9 9.9 %collective-permute-done.2 = bf16[128,2048]{1,0:T(8,128)(2,1)} collective-permute-done((bf16[128,2048]{1,0:T(8,128)(2,1)}, bf16[128,2048]{1,0:T(8,128)(2,1)}, u32[]{:S(2)}, u32[]{:S(2)}) %collective-permute-start.2) | collective-permute-done | bytes 524320 | tf_op jit(solution)/shard_map/ppermute | solution.py:189
  60.8 2.0 %add_convert_fusion.4 = bf16[128,2048]{1,0:T(8,128)(2,1)} fusion(bf16[128,2048]{1,0:T(8,128)(2,1)} %collective-permute-done.2, bf16[512,2048]{1,0:T(8,128)(2,1)S(1)} %copy-done, s32[]{:T(128)S(6)} %select_n.47), kind=kLoop, calls=%fused_computation.4 | loop fusion | flops 1048576 | bytes 1572868 | tf_op jit(solution)/shard_map/convert_element_type | solution.py:187
  62.7 5.2 %collective-permute-start.3 = (bf16[128,2048]{1,0:T(8,128)(2,1)}, bf16[128,2048]{1,0:T(8,128)(2,1)}, u32[]{:S(2)}, u32[]{:S(2)}) collective-permute-start(bf16[128,2048]{1,0:T(8,128)(2,1)} %add_convert_fusion.4), channel_id=1, source_target_pairs={{0,1},{1,2},{4,5},{5,6},{8,9},{9,10},{12,13},{13,14},{16,17},{17,1... | collective-permute-start | bytes 1572872 | tf_op jit(solution)/shard_map/ppermute | solution.py:189
  67.9 10.5 %collective-permute-done.3 = bf16[128,2048]{1,0:T(8,128)(2,1)} collective-permute-done((bf16[128,2048]{1,0:T(8,128)(2,1)}, bf16[128,2048]{1,0:T(8,128)(2,1)}, u32[]{:S(2)}, u32[]{:S(2)}) %collective-permute-start.3) | collective-permute-done | bytes 524320 | tf_op jit(solution)/shard_map/ppermute | solution.py:189
  78.5 2.6 %add_convert_fusion.3 = (bf16[128,2048]{1,0:T(8,128)(2,1)}, bf16[128,2048]{1,0:T(8,128)(2,1)}) fusion(bf16[128,2048]{1,0:T(8,128)(2,1)} %collective-permute-done.3, bf16[512,2048]{1,0:T(8,128)(2,1)S(1)} %copy-done, s32[]{:T(128)S(6)} %select_n.46, bf16[128,2048]{1,0:T(8,128)(2,1)} %collective-permute-done.5, s32[]{:T(128)S(6)} %select_n.50), kind=kLoop, calls=%fused_computation.3 | loop fusion | flops 2097152 | bytes 3145736 | tf_op jit(solution)/shard_map/convert_element_type | solution.py:187
  82.5 3.0 %shard_map.200 = bf16[8,256,256]{2,1,0:T(8,128)(2,1)} custom-call(s32[8]{0:T(128)} %owner.1, bf16[8,256,256]{2,1,0:T(8,128)(2,1)} %copy-done.1), custom_call_target="tpu_custom_call" | custom-call | flops 1024 | bytes 2097152 | tf_op jit(solution)/shard_map/pallas_call | solution.py:37
  85.5 3.7 %all-to-all-start.1 = ((bf16[8,256,256]{2,1,0:T(8,128)(2,1)}), bf16[8,256,256]{2,1,0:T(8,128)(2,1)S(1)}, u32[]{:S(2)}, u32[]{:S(2)}) async-start(bf16[8,256,256]{2,1,0:T(8,128)(2,1)} %shard_map.200), calls=%async_computation.1 | async-start | bytes 2097152 | tf_op jit(solution)/shard_map/all_to_all | solution.py:385
  89.2 5.1 %collective-permute-start.4 = (bf16[128,2048]{1,0:T(8,128)(2,1)}, bf16[128,2048]{1,0:T(8,128)(2,1)}, u32[]{:S(2)}, u32[]{:S(2)}) collective-permute-start(bf16[128,2048]{1,0:T(8,128)(2,1)} %get-tuple-element.20), channel_id=1, source_target_pairs={{0,1},{1,2},{2,3},{4,5},{5,6},{6,7},{8,9},{9,10},{10,11},{12,13},{... | collective-permute-start | bytes 1572872 | tf_op jit(solution)/shard_map/ppermute | solution.py:189
  94.3 2.0 %add_convert_fusion.1 = bf16[128,2048]{1,0:T(8,128)(2,1)} fusion(bf16[128,2048]{1,0:T(8,128)(2,1)} %collective-permute-done.6, bf16[512,2048]{1,0:T(8,128)(2,1)S(1)} %copy-done, s32[]{:T(128)S(6)} %select_n.49), kind=kLoop, calls=%fused_computation.1 | loop fusion | flops 1048576 | bytes 1572868 | tf_op jit(solution)/shard_map/convert_element_type | solution.py:188
  98.5 3.2 %shard_map.194.base = f32[128,2048]{1,0:T(8,128)} custom-call(s32[1]{0:T(128)} %bitcast.place, bf16[512,2048]{1,0:T(8,128)(2,1)} %hidden.3, f32[1,2048]{1,0:T(1,128)} %bitcast.24, bf16[2048,64]{1,0:T(8,128)(2,1)} %copy.21.left, bf16[64,2048]{1,0:T(8,128)(2,1)} %right.1, f32[1,2048]{1,0:T(1,128)} %bitcast.25), custom_call_target="tpu_custom_call" | custom-call | flops 268435456 | bytes 4194304 | tf_op jit(solution)/shard_map/pallas_call | solution.py:37
  101.7 2.8 %all-to-all-done.1 = bf16[8,256,256]{2,1,0:T(8,128)(2,1)S(1)} async-done(((bf16[8,256,256]{2,1,0:T(8,128)(2,1)}), bf16[8,256,256]{2,1,0:T(8,128)(2,1)S(1)}, u32[]{:S(2)}, u32[]{:S(2)}) %all-to-all-start.1) | async-done | bytes 1048608 | tf_op jit(solution)/shard_map/all_to_all | solution.py:385
  105.4 7.1 %collective-permute-done.7 = bf16[128,2048]{1,0:T(8,128)(2,1)} collective-permute-done((bf16[128,2048]{1,0:T(8,128)(2,1)}, bf16[128,2048]{1,0:T(8,128)(2,1)}, u32[]{:S(2)}, u32[]{:S(2)}) %collective-permute-start.7) | collective-permute-done | bytes 524320 | tf_op jit(solution)/shard_map/ppermute | solution.py:190
  112.5 2.2 %add_convert_fusion.proj = bf16[128,2048]{1,0:T(8,128)(2,1)} fusion(bf16[128,2048]{1,0:T(8,128)(2,1)} %collective-permute-done.7, bf16[128,2048]{1,0:T(8,128)(2,1)} %collective-permute-done.4, bf16[512,2048]{1,0:T(8,128)(2,1)S(1)} %copy-done, s32[]{:T(128)S(6)} %select_n.45), kind=kLoop, calls=%fused_computation | loop fusion | flops 1572864 | bytes 2097156 | tf_op jit(solution)/shard_map/convert_element_type | solution.py:192
  114.8 4.0 %shard_map.199 = bf16[128,2048]{1,0:T(8,128)(2,1)} custom-call(f32[128,2048]{1,0:T(8,128)} %shard_map.194.base, bf16[128,2048]{1,0:T(8,128)(2,1)} %add_convert_fusion.proj, f32[1,2048]{1,0:T(1,128)} %bitcast.26, bf16[128,256]{1,0:T(8,128)(2,1)} %layer_input.1, bf16[2048,256]{1,0:T(8,128)(2,1)} %w_plgate.1, bf16[256,2048]{1,0:T(8,128)(2,1)} %w_plproj.1, ...), custom_call_target="tpu_custom_call" | custom-call | flops 268435456 | bytes 6291456 | tf_op jit(solution)/shard_map/pallas_call | solution.py:37
  (26 shorter events, 9.1 us)
Async XLA Ops:
  9.0 24.4 %collective-permute-start = (bf16[512,256]{1,0:T(8,128)(2,1)}, bf16[512,256]{1,0:T(8,128)(2,1)S(1)}, u32[]{:S(2)}, u32[]{:S(2)}) collective-permute-start(bf16[512,256]{1,0:T(8,128)(2,1)} %get-tuple-element.12.fresh.own), channel_id=1, source_target_pairs={{0,1},{1,2},{2,0},{4,5},{5,6},{6,4},{8,9},{9,10},{10,8},{12,13},{1... | collective-permute-start | bytes 786440 | tf_op jit(solution)/shard_map/ppermute | solution.py:269
  13.9 19.5 %collective-permute-start.1 = (bf16[512,256]{1,0:T(8,128)(2,1)}, bf16[512,256]{1,0:T(8,128)(2,1)S(1)}, u32[]{:S(2)}, u32[]{:S(2)}) collective-permute-start(bf16[512,256]{1,0:T(8,128)(2,1)} %get-tuple-element.12.fresh.own), channel_id=1, source_target_pairs={{1,3},{2,1},{3,2},{5,7},{6,5},{7,6},{9,11},{10,9},{11,10},{13,15},... | collective-permute-start | bytes 786440 | tf_op jit(solution)/shard_map/ppermute | solution.py:270
  19.3 22.0 %all-to-all-start = ((bf16[8,256,256]{2,1,0:T(8,128)(2,1)}), bf16[8,256,256]{2,1,0:T(8,128)(2,1)S(1)}, u32[]{:S(2)}, u32[]{:S(2)}) async-start(bf16[8,256,256]{2,1,0:T(8,128)(2,1)} %bitcast.21), calls=%async_computation | async-start | bytes 2097152 | tf_op jit(solution)/shard_map/all_to_all | solution.py:293
  33.4 0.7 copy-start.3
  33.4 0.8 copy-start.4
  41.2 19.6 %copy-start = (bf16[512,2048]{1,0:T(8,128)(2,1)S(1)}, bf16[512,2048]{1,0:T(8,128)(2,1)}, u32[]{:S(2)}) copy-start(bf16[512,2048]{1,0:T(8,128)(2,1)} %shard_map.198) | copy-start | bytes 6291460
  41.2 39.8 %copy-start.1 = (bf16[8,256,256]{2,1,0:T(8,128)(2,1)}, bf16[8,256,256]{2,1,0:T(8,128)(2,1)S(1)}, u32[]{:S(2)}) copy-start(bf16[8,256,256]{2,1,0:T(8,128)(2,1)S(1)} %all-to-all-done.spread) | copy-start | bytes 3145732
  43.9 16.8 %collective-permute-start.2 = (bf16[128,2048]{1,0:T(8,128)(2,1)}, bf16[128,2048]{1,0:T(8,128)(2,1)}, u32[]{:S(2)}, u32[]{:S(2)}) collective-permute-start(bf16[128,2048]{1,0:T(8,128)(2,1)} %get-tuple-element.22), channel_id=1, source_target_pairs={{0,1},{4,5},{8,9},{12,13},{16,17},{20,21},{24,25},{28,29}} | collective-permute-start | bytes 1572872 | tf_op jit(solution)/shard_map/ppermute | solution.py:189
  49.4 18.5 %collective-permute-start.5 = (bf16[128,2048]{1,0:T(8,128)(2,1)}, bf16[128,2048]{1,0:T(8,128)(2,1)}, u32[]{:S(2)}, u32[]{:S(2)}) collective-permute-start(bf16[128,2048]{1,0:T(8,128)(2,1)} %get-tuple-element.23), channel_id=1, source_target_pairs={{3,2},{7,6},{11,10},{15,14},{19,18},{23,22},{27,26},{31,30}} | collective-permute-start | bytes 1572872 | tf_op jit(solution)/shard_map/ppermute | solution.py:190
  62.7 15.7 %collective-permute-start.3 = (bf16[128,2048]{1,0:T(8,128)(2,1)}, bf16[128,2048]{1,0:T(8,128)(2,1)}, u32[]{:S(2)}, u32[]{:S(2)}) collective-permute-start(bf16[128,2048]{1,0:T(8,128)(2,1)} %add_convert_fusion.4), channel_id=1, source_target_pairs={{0,1},{1,2},{4,5},{5,6},{8,9},{9,10},{12,13},{13,14},{16,17},{17,1... | collective-permute-start | bytes 1572872 | tf_op jit(solution)/shard_map/ppermute | solution.py:189
  81.0 13.2 %collective-permute-start.6 = (bf16[128,2048]{1,0:T(8,128)(2,1)}, bf16[128,2048]{1,0:T(8,128)(2,1)}, u32[]{:S(2)}, u32[]{:S(2)}) collective-permute-start(bf16[128,2048]{1,0:T(8,128)(2,1)} %get-tuple-element.21), channel_id=1, source_target_pairs={{3,2},{2,1},{7,6},{6,5},{11,10},{10,9},{15,14},{14,13},{19,18},{18... | collective-permute-start | bytes 1572872 | tf_op jit(solution)/shard_map/ppermute | solution.py:190
  85.5 12.1 %copy-start.2 = (bf16[2048,64]{0,1:T(8,128)(2,1)S(1)}, bf16[2048,64]{0,1:T(8,128)(2,1)}, u32[]{:S(2)}) copy-start(bf16[2048,64]{0,1:T(8,128)(2,1)} %param.28) | copy-start | bytes 786436
  85.5 19.0 %all-to-all-start.1 = ((bf16[8,256,256]{2,1,0:T(8,128)(2,1)}), bf16[8,256,256]{2,1,0:T(8,128)(2,1)S(1)}, u32[]{:S(2)}, u32[]{:S(2)}) async-start(bf16[8,256,256]{2,1,0:T(8,128)(2,1)} %shard_map.200), calls=%async_computation.1 | async-start | bytes 2097152 | tf_op jit(solution)/shard_map/all_to_all | solution.py:385
  89.2 16.3 %collective-permute-start.4 = (bf16[128,2048]{1,0:T(8,128)(2,1)}, bf16[128,2048]{1,0:T(8,128)(2,1)}, u32[]{:S(2)}, u32[]{:S(2)}) collective-permute-start(bf16[128,2048]{1,0:T(8,128)(2,1)} %get-tuple-element.20), channel_id=1, source_target_pairs={{0,1},{1,2},{2,3},{4,5},{5,6},{6,7},{8,9},{9,10},{10,11},{12,13},{... | collective-permute-start | bytes 1572872 | tf_op jit(solution)/shard_map/ppermute | solution.py:189
  96.2 16.3 %collective-permute-start.7 = (bf16[128,2048]{1,0:T(8,128)(2,1)}, bf16[128,2048]{1,0:T(8,128)(2,1)}, u32[]{:S(2)}, u32[]{:S(2)}) collective-permute-start(bf16[128,2048]{1,0:T(8,128)(2,1)} %add_convert_fusion.1), channel_id=1, source_target_pairs={{3,2},{2,1},{1,0},{7,6},{6,5},{5,4},{11,10},{10,9},{9,8},{15,14},{... | collective-permute-start | bytes 1572872 | tf_op jit(solution)/shard_map/ppermute | solution.py:190
